TPU v7x, 32 devices: a whole 2x2x4 slice. The times are simulated.
32 devices in a mesh: seq: 16 (over z, y, core), head: 2 (over x).
Axes of the slice: x: 2, y: 2, z: 4, core: 2. Of those that a mesh axis runs over, the one named last changes fastest.
Arguments:
- queries: bfloat16 [4096, 4096], P('seq', 'head'), may hold values from -0.29882812 to 0.29882812
- keys: bfloat16 [4096, 4096], P('seq', 'head'), may hold values from -0.29882812 to 0.29882812
- values: bfloat16 [4096, 4096], P('seq', 'head'), may hold values from -0.59765625 to 0.59765625
- out_grad: bfloat16 [4096, 4096], P('seq', 'head'), may hold values from -6 to 6
- doc_lengths: int32 [8], replicated, may hold values from 1 to 1024, 4096 in all
Outputs:
- query_grad: bfloat16 [4096, 4096], P(('seq', 'head'))
- key_grad: bfloat16 [4096, 4096], P(('seq', 'head'))
- value_grad: bfloat16 [4096, 4096], P(('seq', 'head'))
Inputs may be any that keep to these rules, and one draw needn't show every extreme that they name: `doc_lengths`: the lengths sum to 4096 and the largest equals 1024.
All inputs are finite; a program needn't handle non-finite values.
Results may differ from a plain program's by a relative error of at most 0.0033.
Values may be sent and summed in bfloat16 or wider, within the bound.
No kernel may reach another device: no remote copies, remote signals or barrier semaphores. Data moves between devices by JAX's collectives and lax.ppermute only.
A program may use at most 128 MiB of HBM per device.

v0:
```python
import jax
import jax.numpy as jnp
from jax import lax
from jax.sharding import PartitionSpec as P

HEAD_DIM = 128


def prefix(part, axis, combine, identity, reverse):
    count = lax.axis_size(axis)
    place = lax.axis_index(axis)
    ahead = count - 1 - place if reverse else place
    gathered = jax.tree.map(lambda a: lax.all_gather(a, axis), part)
    state = jax.tree.map(lambda a, e: jnp.zeros_like(a) + jnp.asarray(e, a.dtype), part, identity)

    def one(lap, state):
        source = count - 1 - lap if reverse else lap
        return combine(
            state, jax.tree.map(lambda a: lax.dynamic_index_in_dim(a, source, 0, False), gathered)
        )

    return lax.fori_loop(0, ahead, one, state)


def combine_pair(earlier, current):
    return (current[0] + (1.0 - current[1]) * earlier[0], jnp.maximum(earlier[1], current[1]))


def shards(queries, keys, values, out_grad, doc_lengths):
    rows_dev = queries.shape[0]
    width = queries.shape[1]
    head_count = width // HEAD_DIM
    shard_begin = lax.axis_index("seq") * rows_dev
    starts = jnp.cumsum(doc_lengths) - doc_lengths
    order = jnp.arange(rows_dev, dtype=jnp.int32)
    position = shard_begin + order
    before = starts[None, :] <= position[:, None]
    doc_index = jnp.sum(before.astype(jnp.int32), axis=1) - 1
    doc_begin = jnp.max(jnp.where(before, starts[None, :], 0), axis=1)
    first_rows = doc_begin < shard_begin
    last_rows = doc_index == doc_index[rows_dev - 1]
    has_start = jnp.any(doc_begin >= shard_begin).astype(jnp.float32)
    query_heads = queries.reshape(rows_dev, head_count, HEAD_DIM)
    key_heads = keys.reshape(rows_dev, head_count, HEAD_DIM)
    value_heads = values.reshape(rows_dev, head_count, HEAD_DIM)
    grad_heads = out_grad.reshape(rows_dev, head_count, HEAD_DIM)
    tail_keys = jnp.where(last_rows[:, None, None], key_heads, jnp.zeros_like(key_heads))
    tail_state = jnp.einsum(
        "lhd,lhe->hde", tail_keys, value_heads, preferred_element_type=jnp.float32
    )
    head_queries = jnp.where(first_rows[:, None, None], query_heads, jnp.zeros_like(query_heads))
    head_state = jnp.einsum(
        "lhd,lhe->hde", head_queries, grad_heads, preferred_element_type=jnp.float32
    )
    empty = (jnp.zeros((head_count, HEAD_DIM, HEAD_DIM), jnp.float32), jnp.zeros((), jnp.float32))
    state_in = prefix((tail_state, has_start), "seq", combine_pair, empty, False)[0]
    grad_in = prefix((head_state, has_start), "seq", combine_pair, empty, True)[0]
    pair_mask = (doc_index[:, None] == doc_index[None, :]) & (order[:, None] >= order[None, :])
    score_qk = jnp.einsum(
        "thd,shd->hts", query_heads, key_heads, preferred_element_type=jnp.float32
    )
    weight_qk = jnp.where(pair_mask[None], score_qk, 0.0).astype(jnp.bfloat16)
    score_gv = jnp.einsum(
        "the,she->hts", grad_heads, value_heads, preferred_element_type=jnp.float32
    )
    weight_gv = jnp.where(pair_mask[None], score_gv, 0.0).astype(jnp.bfloat16)
    high = lax.Precision.HIGHEST
    carry_query = jnp.einsum(
        "hde,the->thd", state_in, grad_heads.astype(jnp.float32), precision=high
    )
    query_local = jnp.einsum(
        "hts,shd->thd", weight_gv, key_heads, preferred_element_type=jnp.float32
    )
    query_out = (
        (query_local + jnp.where(first_rows[:, None, None], carry_query, 0.0))
        .reshape(rows_dev, width)
        .astype(jnp.bfloat16)
    )
    carry_key = jnp.einsum("hde,she->shd", grad_in, value_heads.astype(jnp.float32), precision=high)
    carry_value = jnp.einsum("hde,shd->she", grad_in, key_heads.astype(jnp.float32), precision=high)
    key_local = jnp.einsum(
        "hts,thd->shd", weight_gv, query_heads, preferred_element_type=jnp.float32
    )
    value_local = jnp.einsum(
        "hts,the->she", weight_qk, grad_heads, preferred_element_type=jnp.float32
    )
    key_out = (
        (key_local + jnp.where(last_rows[:, None, None], carry_key, 0.0))
        .reshape(rows_dev, width)
        .astype(jnp.bfloat16)
    )
    value_out = (
        (value_local + jnp.where(last_rows[:, None, None], carry_value, 0.0))
        .reshape(rows_dev, width)
        .astype(jnp.bfloat16)
    )
    query_grad, key_grad, value_grad = (
        lax.all_to_all(query_out, "head", split_axis=0, concat_axis=1, tiled=True),
        lax.all_to_all(key_out, "head", split_axis=0, concat_axis=1, tiled=True),
        lax.all_to_all(value_out, "head", split_axis=0, concat_axis=1, tiled=True),
    )
    return (query_grad, key_grad, value_grad)


def solution(mesh):
    return jax.shard_map(
        shards,
        mesh=mesh,
        in_specs=(P("seq", "head"), P("seq", "head"), P("seq", "head"), P("seq", "head"), P()),
        out_specs=(P(("seq", "head"), None), P(("seq", "head"), None), P(("seq", "head"), None)),
        check_vma=False,
    )
```

profile of v0, /device:TPU:29, one launch (start us, length us, event | category | flops | bytes accessed | tf_op | source)
XLA Modules:
  0.0 357.8 jit_solution(1843559602949527739)
XLA Ops:
  7.2 0.9 reduce-window.9
  8.2 0.7 bitcast_subtract_fusion
  8.9 0.6 broadcast_compare_fusion.1
  9.5 1.5 copy.141
  11.0 1.4 fusion.9
  13.1 1.5 copy.140
  14.6 0.7 broadcast_compare_fusion
  15.2 2.6 fusion.5
  19.0 0.7 dynamic-update-slice
  19.7 30.0 %all-reduce = f32[16]{0:T(128)S(1)} all-reduce(f32[16]{0:T(128)S(1)} %dynamic-update-slice), channel_id=1, replica_groups=mesh['seq'=16,'head'=2] {'seq'}, use_global_device_ids=true, to_apply=%add | all-reduce | flops 16 | bytes 128
  49.8 1.9 select_convert_fusion.1
  51.8 1.3 copy-done.1
  53.1 2.1 fusion.32
  55.2 2.6 fusion.3
  57.8 80.4 %all-gather.7.cloned.1.call-done = f32[256,128,128]{2,1,0:T(8,128)} async-done(((f32[16,128,128]{2,1,0:T(8,128)}), f32[256,128,128]{2,1,0:T(8,128)}) %all-gather.7.cloned.1.call-update) | async-done | bytes 16777232 | tf_op jit(solution)/shard_map/all_gather | solution.py:13
  138.4 3.0 fusion
  141.4 0.7 copy.129
  142.0 1.3 convert_element_type.42
  143.3 4.4 %all-to-all-start.2 = ((bf16[2,128,2048]{2,1,0:T(8,128)(2,1)}), bf16[2,128,2048]{2,1,0:T(8,128)(2,1)}, u32[]{:S(2)}, u32[]{:S(2)}) async-start(bf16[2,128,2048]{2,1,0:T(8,128)(2,1)} %convert_element_type.42), calls=%async_computation.2 | async-start | bytes 2097152 | tf_op jit(solution)/shard_map/all_to_all | solution.py:100
  147.7 118.3 %all-gather.5.cloned.1.call-done = f32[256,128,128]{2,1,0:T(8,128)} async-done(((f32[16,128,128]{2,1,0:T(8,128)}), f32[256,128,128]{2,1,0:T(8,128)}) %all-gather.5.cloned.1.call-update) | async-done | bytes 16777232 | tf_op jit(solution)/shard_map/all_gather | solution.py:13
  266.2 43.5 %while.26 = (s32[]{:T(128)}, f32[16,128,128]{2,1,0:T(8,128)S(1)}, s32[]{:T(128)}, f32[16,16,128,128]{3,2,1,0:T(8,128)}, f32[16]{0:T(128)S(1)}, /*index=5*/s32[]{:T(128)}, s32[]{:T(128)}, s32[]{:T(128)}, f32[1]{0:T(128)}) while((s32[]{:T(128)}, f32[16,128,128]{2,1,0:T(8,128)S(1)}, s32[]{:T(128)}, f32[16,16,128,128]{3,2,1,0:T(8,128)}, ...), condition=%wide.region_5.6_spmd, body=%wide.region_4.5_spmd.sunk | while | flops 524294 | bytes 3145887 | solution.py:22
  266.2 0.6 dynamic_slice.33
  267.4 1.6 bitcast_add_fusion.7
  269.1 0.6 dynamic_slice.33
  270.3 1.6 bitcast_add_fusion.7
  272.0 0.6 dynamic_slice.33
  273.2 1.6 bitcast_add_fusion.7
  274.9 0.6 dynamic_slice.33
  276.1 1.6 bitcast_add_fusion.7
  277.8 0.6 dynamic_slice.33
  279.0 1.6 bitcast_add_fusion.7
  280.7 0.6 dynamic_slice.33
  281.9 1.6 bitcast_add_fusion.7
  283.6 0.6 dynamic_slice.33
  284.8 1.6 bitcast_add_fusion.7
  286.5 0.6 dynamic_slice.33
  287.7 1.6 bitcast_add_fusion.7
  289.4 0.6 dynamic_slice.33
  290.6 1.6 bitcast_add_fusion.7
  292.3 0.6 dynamic_slice.33
  293.5 1.6 bitcast_add_fusion.7
  296.4 1.6 bitcast_add_fusion.7
  299.3 1.6 bitcast_add_fusion.7
  302.2 1.6 bitcast_add_fusion.7
  303.9 0.6 dynamic_slice.33
  305.1 1.6 bitcast_add_fusion.7
  308.0 1.6 bitcast_add_fusion.7
  309.7 2.7 fusion.2
  312.4 1.6 copy.112
  314.0 2.4 convert_element_type.37
  316.4 4.6 %all-to-all-start = ((bf16[2,128,2048]{2,1,0:T(8,128)(2,1)}), bf16[2,128,2048]{2,1,0:T(8,128)(2,1)}, u32[]{:S(2)}, u32[]{:S(2)}) async-start(bf16[2,128,2048]{2,1,0:T(8,128)(2,1)} %convert_element_type.37), calls=%async_computation | async-start | bytes 2097152 | tf_op jit(solution)/shard_map/all_to_all | solution.py:98
  321.1 2.4 fusion.33
  323.5 1.2 fusion.1
  324.8 0.7 copy.120
  325.4 1.3 convert_element_type.39
  326.7 5.9 %all-to-all-done = bf16[2,128,2048]{2,1,0:T(8,128)(2,1)} async-done(((bf16[2,128,2048]{2,1,0:T(8,128)(2,1)}), bf16[2,128,2048]{2,1,0:T(8,128)(2,1)}, u32[]{:S(2)}, u32[]{:S(2)}) %all-to-all-start) | async-done | bytes 1048608 | tf_op jit(solution)/shard_map/all_to_all | solution.py:98
  332.6 3.6 %all-to-all-start.1 = ((bf16[2,128,2048]{2,1,0:T(8,128)(2,1)}), bf16[2,128,2048]{2,1,0:T(8,128)(2,1)S(1)}, u32[]{:S(2)}, u32[]{:S(2)}) async-start(bf16[2,128,2048]{2,1,0:T(8,128)(2,1)} %convert_element_type.39), calls=%async_computation.1 | async-start | bytes 2097152 | tf_op jit(solution)/shard_map/all_to_all | solution.py:99
  336.2 1.6 copy.130
  337.8 1.3 copy.133
  339.1 1.6 copy.113
  340.8 1.3 copy.131
  342.1 6.9 %all-to-all-done.1 = bf16[2,128,2048]{2,1,0:T(8,128)(2,1)S(1)} async-done(((bf16[2,128,2048]{2,1,0:T(8,128)(2,1)}), bf16[2,128,2048]{2,1,0:T(8,128)(2,1)S(1)}, u32[]{:S(2)}, u32[]{:S(2)}) %all-to-all-start.1) | async-done | bytes 1048608 | tf_op jit(solution)/shard_map/all_to_all | solution.py:99
  348.9 0.7 copy.121
  349.6 1.3 copy.132
  (30 shorter events, 4.0 us)
Async XLA Ops:
  7.2 3.8 %copy-start = (bf16[256,2048]{1,0:T(8,128)(2,1)S(1)}, bf16[256,2048]{1,0:T(8,128)(2,1)}, u32[]{:S(2)}) copy-start(bf16[256,2048]{1,0:T(8,128)(2,1)} %param.12) | copy-start | bytes 3145732
  7.2 131.1 %all-gather.7.cloned.1.call-start = ((), (), s32[]{:S(2)}) async-start(), calls=%async_computation.4 | async-start | bytes 17825792 | tf_op jit(solution)/shard_map/all_gather | solution.py:13
  11.0 44.2 %copy-start.2 = (bf16[256,2048]{0,1:T(8,128)(2,1)}, bf16[256,2048]{0,1:T(8,128)(2,1)S(1)}, u32[]{:S(2)}) copy-start(bf16[256,2048]{0,1:T(8,128)(2,1)S(1)} %copy.141) | copy-start | bytes 3145732
  12.4 253.6 %all-gather.5.cloned.1.call-start = ((), (), s32[]{:S(2)}) async-start(), calls=%async_computation.3 | async-start | bytes 17825792 | tf_op jit(solution)/shard_map/all_gather | solution.py:13
  15.2 3.2 copy-start.5
  51.7 1.3 copy-start.1
  143.3 173.1 %all-to-all-start.2 = ((bf16[2,128,2048]{2,1,0:T(8,128)(2,1)}), bf16[2,128,2048]{2,1,0:T(8,128)(2,1)}, u32[]{:S(2)}, u32[]{:S(2)}) async-start(bf16[2,128,2048]{2,1,0:T(8,128)(2,1)} %convert_element_type.42), calls=%async_computation.2 | async-start | bytes 2097152 | tf_op jit(solution)/shard_map/all_to_all | solution.py:100
  314.0 7.0 %copy-start.3 = (bf16[256,2048]{0,1:T(8,128)(2,1)S(1)}, bf16[256,2048]{0,1:T(8,128)(2,1)}, u32[]{:S(2)}) copy-start(bf16[256,2048]{0,1:T(8,128)(2,1)} %copy-done.2) | copy-start | bytes 3145732
  316.4 16.2 %all-to-all-start = ((bf16[2,128,2048]{2,1,0:T(8,128)(2,1)}), bf16[2,128,2048]{2,1,0:T(8,128)(2,1)}, u32[]{:S(2)}, u32[]{:S(2)}) async-start(bf16[2,128,2048]{2,1,0:T(8,128)(2,1)} %convert_element_type.37), calls=%async_computation | async-start | bytes 2097152 | tf_op jit(solution)/shard_map/all_to_all | solution.py:98
  321.1 2.5 copy-start.4
  332.6 16.3 %all-to-all-start.1 = ((bf16[2,128,2048]{2,1,0:T(8,128)(2,1)}), bf16[2,128,2048]{2,1,0:T(8,128)(2,1)S(1)}, u32[]{:S(2)}, u32[]{:S(2)}) async-start(bf16[2,128,2048]{2,1,0:T(8,128)(2,1)} %convert_element_type.39), calls=%async_computation.1 | async-start | bytes 2097152 | tf_op jit(solution)/shard_map/all_to_all | solution.py:99
Sparse Core Ops, SparseCore 0:
  12.6 125.6 all-gather.6
  141.0 125.0 all-gather.4
where the time goes:
time: 359 us; the launch traced here: 358 us
  waiting for transfers between devices  212 us (59%)
  local copies, waits for them, and re-layouts  30.8 us (9%)
  blocking collectives  30 us (8%)
  other arithmetic  27.5 us (8%)
  matrix products  20.1 us (6%)
  between operations  14.9 us (4%)
  starting transfers between devices  12.7 us (4%)
  loops' own time  10.2 us (3%)
    all_gather x2, waiting for transfers between devices, prefix(): gathered = jax.tree.map(lambda a: lax.all_gather(a, axis), part)  199 us
    unnamed x1, blocking collectives  30 us
    add x15, other arithmetic, combine_pair(): current[0] + (1.0 - current[1]) * earlier[0]  24.5 us
    another operation x2, loops' own time, prefix(): return lax.fori_loop(0, ahead, one, state)  10.2 us
    dynamic_slice x15, local copies, waits for them, and re-layouts, one(): lax.dynamic_index_in_dim(a, source, 0, False)  8.8 us
  transfers between devices with their start and end apart: 5, of which 4 were waited for; matrix products, arithmetic and copies ran while one was open for 20% of the time, Pallas kernels for 0%

commit v1 on v0

v1 whole, which is shorter than its diff:
```python
import functools

import jax
import jax.numpy as jnp
from jax import lax
from jax.experimental import pallas as pl
from jax.experimental.pallas import tpu as pltpu
from jax.sharding import PartitionSpec as P

HEAD_DIM = 128
MOST = 1024
CHUNKS = 2
VMEM_LIMIT = 48 * 1024 * 1024
NT = (((1,), (1,)), ((), ()))
TN = (((0,), (0,)), ((), ()))
NN = (((1,), (0,)), ((), ()))


def dot(a, b, dims):
    return lax.dot_general(a, b, dims, preferred_element_type=jnp.float32)


def doc_at(meta, ndocs, position):
    start, begin, end = jnp.int32(0), jnp.int32(0), jnp.int32(0)
    for i in range(ndocs):
        stop = start + meta[i]
        begin = jnp.where(start <= position, start, begin)
        end = jnp.where(start <= position, stop, end)
        start = stop
    return begin, end


def block_range(meta, ndocs, base, rows):
    begin0, end0 = doc_at(meta, ndocs, base)
    begin1, end1 = doc_at(meta, ndocs, base + rows - 1)
    first = jnp.where(begin0 < base, end0, base) - base
    return begin0, end0, begin1, end1, first, begin1 - base


def pack_kernel(meta, q, k, v, g, out, sems, *, ndocs, half):
    other = 1 - lax.rem(meta[ndocs], 2)
    copies = []
    for i, ref in enumerate((q, k, v, g)):
        src = ref.at[:, pl.ds(pl.multiple_of(other * half, 128), half)]
        copies.append(pltpu.make_async_copy(src, out.at[i], sems.at[i]))
        copies[-1].start()
    for copy in copies:
        copy.wait()


def state_kernel(meta, q, k, v, g, pair, tail_out, head_out, even_tail, odd_head, *, ndocs, rows, heads):
    place = meta[ndocs]
    odd_here = lax.rem(place, 2) == 1
    even = (place - lax.rem(place, 2)) * rows
    odd = even + rows
    even_b0, even_e0, _, _, even_first, even_last = block_range(meta, ndocs, even, rows)
    _, _, odd_b1, _, odd_first, odd_last = block_range(meta, ndocs, odd, rows)
    order = lax.broadcasted_iota(jnp.int32, (rows, HEAD_DIM), 0)
    own_first = jnp.where(odd_here, odd_first, even_first)
    own_last = jnp.where(odd_here, odd_last, even_last)
    far_first = jnp.where(odd_here, even_first, odd_first)
    far_last = jnp.where(odd_here, even_last, odd_last)
    tail_joins = jnp.where(odd_b1 < odd, 1.0, 0.0)
    head_joins = jnp.where(even_e0 > odd, 1.0, 0.0)
    zero = jnp.zeros((), q.dtype)
    for h in range(heads):
        cols = slice(h * HEAD_DIM, (h + 1) * HEAD_DIM)
        own_tail = dot(jnp.where(order >= own_last, k[:, cols], zero), v[:, cols], TN)
        far_tail = dot(jnp.where(order >= far_last, pair[1, :, cols], zero), pair[2, :, cols], TN)
        own_head = dot(jnp.where(order < own_first, q[:, cols], zero), g[:, cols], TN)
        far_head = dot(jnp.where(order < far_first, pair[0, :, cols], zero), pair[3, :, cols], TN)
        tail_even = jnp.where(odd_here, far_tail, own_tail)
        tail_odd = jnp.where(odd_here, own_tail, far_tail)
        head_even = jnp.where(odd_here, far_head, own_head)
        head_odd = jnp.where(odd_here, own_head, far_head)
        tail_out[h] = tail_odd + tail_joins * tail_even
        head_out[h] = head_even + head_joins * head_odd
        even_tail[h] = tail_even
        odd_head[h] = head_odd


def split(a):
    high = a.astype(jnp.bfloat16)
    return high, (a - high.astype(jnp.float32)).astype(jnp.bfloat16)


def grad_kernel(meta, q, k, v, g, pair, even_tail, odd_head, tails, heads_in, *rest, ndocs, rows, heads, groups, hops):
    outs, (done,) = rest[:-1], rest[-1:]
    place, column = meta[ndocs], meta[ndocs + 1]
    odd_here = lax.rem(place, 2) == 1
    even = (place - lax.rem(place, 2)) * rows
    odd = even + rows
    even_range = block_range(meta, ndocs, even, rows)
    odd_range = block_range(meta, ndocs, odd, rows)
    even_b0, even_e1 = even_range[0], even_range[3]
    odd_b0, odd_e1 = odd_range[0], odd_range[3]

    def one(flag):
        return jnp.where(flag, 1.0, 0.0)

    tail_w = [one(even - hop * 2 * rows > even_b0) for hop in range(hops)]
    head_w = [one(odd + rows + hop * 2 * rows < odd_e1) for hop in range(hops)]
    state_from_tail, state_from_pair = one(odd > odd_b0), one(even > odd_b0)
    grad_from_head, grad_from_pair = one(odd < even_e1), one(odd + rows < even_e1)
    order = lax.broadcasted_iota(jnp.int32, (rows, HEAD_DIM), 0)
    line = lax.broadcasted_iota(jnp.int32, (rows, rows), 0)
    across = lax.broadcasted_iota(jnp.int32, (rows, rows), 1)
    sides = []
    for base, first, last in (
        (jnp.where(odd_here, odd, even), jnp.where(odd_here, odd_range[4], even_range[4]), jnp.where(odd_here, odd_range[5], even_range[5])),
        (jnp.where(odd_here, even, odd), jnp.where(odd_here, even_range[4], odd_range[4]), jnp.where(odd_here, even_range[5], odd_range[5])),
    ):
        begin_line = jnp.zeros((rows, rows), jnp.int32)
        begin_across = jnp.zeros((rows, rows), jnp.int32)
        start = jnp.int32(0) - base
        for i in range(ndocs):
            begin_line = jnp.where(line >= start, start, begin_line)
            begin_across = jnp.where(across >= start, start, begin_across)
            start = start + meta[i]
        lower = (across <= line) & (across >= begin_line)
        upper = (line <= across) & (line >= begin_across)
        sides.append((lower, upper, order < first, order >= last))
    for h in range(heads):
        cols = slice(h * HEAD_DIM, (h + 1) * HEAD_DIM)
        state_even = tail_w[0] * tails[0, h]
        grad_odd = head_w[0] * heads_in[0, h]
        for hop in range(1, hops):
            state_even = state_even + tail_w[hop] * tails[hop, h]
            grad_odd = grad_odd + head_w[hop] * heads_in[hop, h]
        state_odd = state_from_tail * even_tail[h] + state_from_pair * state_even
        grad_even = grad_from_head * odd_head[h] + grad_from_pair * grad_odd
        states = (jnp.where(odd_here, state_odd, state_even), jnp.where(odd_here, state_even, state_odd))
        grads = (jnp.where(odd_here, grad_odd, grad_even), jnp.where(odd_here, grad_even, grad_odd))
        for side in range(2):
            lower, upper, first_rows, last_rows = sides[side]
            if side == 0:
                qh, kh, vh, gh = (ref[:, cols] for ref in (q, k, v, g))
            else:
                qh, kh, vh, gh = (pair[i, :, cols] for i in range(4))
            state_hi, state_lo = split(states[side])
            grad_hi, grad_lo = split(grads[side])
            weight_gv = jnp.where(lower, dot(gh, vh, NT), 0.0).astype(jnp.bfloat16)
            weight_vg = jnp.where(upper, dot(vh, gh, NT), 0.0).astype(jnp.bfloat16)
            weight_kq = jnp.where(upper, dot(kh, qh, NT), 0.0).astype(jnp.bfloat16)
            carry_q = dot(gh, state_hi, NT) + dot(gh, state_lo, NT)
            carry_k = dot(vh, grad_hi, NT) + dot(vh, grad_lo, NT)
            carry_v = dot(kh, grad_hi, NN) + dot(kh, grad_lo, NN)
            q_out = dot(weight_gv, kh, NN) + jnp.where(first_rows, carry_q, 0.0)
            k_out = dot(weight_vg, qh, NN) + jnp.where(last_rows, carry_k, 0.0)
            v_out = dot(weight_kq, gh, NN) + jnp.where(last_rows, carry_v, 0.0)
            done[side, 0, :, cols] = q_out.astype(jnp.bfloat16)
            done[side, 1, :, cols] = k_out.astype(jnp.bfloat16)
            done[side, 2, :, cols] = v_out.astype(jnp.bfloat16)
    part = rows // groups
    for side in range(2):
        for j in range(groups):
            target = lax.rem(column + j, groups)
            at = pl.ds(pl.multiple_of(target * part, part), part)
            for i in range(3):
                outs[side * groups + j][i] = done[side, i, at, :]


def place_kernel(meta, *refs, ndocs, groups, chunks, width, half, cw):
    count = 2 * groups * chunks
    parts, outs, sems = refs[:count], refs[count:count + 3], refs[count + 3]
    side_here, column = lax.rem(meta[ndocs], 2), meta[ndocs + 1]
    copies = []
    for c in range(chunks):
        for side in range(2):
            for j in range(groups):
                source = lax.rem(column + groups - j, groups)
                side_from = side_here if side == 0 else 1 - side_here
                start = pl.multiple_of(source * width + side_from * half + c * cw, 128)
                ref = parts[(c * 2 + side) * groups + j]
                for i in range(3):
                    copy = pltpu.make_async_copy(ref.at[i], outs[i].at[:, pl.ds(start, cw)], sems.at[len(copies)])
                    copy.start()
                    copies.append(copy)
    for copy in copies:
        copy.wait()


def shards(queries, keys, values, out_grad, doc_lengths):
    rows, width = queries.shape
    half = width // 2
    ndocs = doc_lengths.shape[0]
    seq, groups = lax.axis_size("seq"), lax.axis_size("head")
    hops = -(-MOST // (2 * rows))
    chunks = min(CHUNKS, half // HEAD_DIM)
    cw = half // chunks
    heads = cw // HEAD_DIM
    part = rows // groups
    meta = jnp.concatenate(
        [doc_lengths, jnp.stack([lax.axis_index("seq"), lax.axis_index("head")]).astype(jnp.int32)]
    )
    params = pltpu.CompilerParams(vmem_limit_bytes=VMEM_LIMIT)
    anywhere = pl.BlockSpec(memory_space=pl.ANY)
    f32, bf16 = jnp.float32, jnp.bfloat16

    packed = pl.pallas_call(
        functools.partial(pack_kernel, ndocs=ndocs, half=half),
        grid_spec=pltpu.PrefetchScalarGridSpec(
            num_scalar_prefetch=1, grid=(1,), in_specs=[anywhere] * 4, out_specs=anywhere,
            scratch_shapes=[pltpu.SemaphoreType.DMA((4,))],
        ),
        out_shape=jax.ShapeDtypeStruct((4, rows, half), bf16),
        cost_estimate=pl.CostEstimate(flops=0, bytes_accessed=16 * rows * half, transcendentals=0),
        compiler_params=params, name="pack",
    )(meta, queries, keys, values, out_grad)
    pair = lax.ppermute(packed, "seq", [(b, b ^ 1) for b in range(seq)])

    square = (heads, HEAD_DIM, HEAD_DIM)
    state_spec = pl.BlockSpec(square, lambda s, meta: (0, 0, 0))
    results = []
    stage = []
    for c in range(chunks):
        own = pl.BlockSpec((rows, cw), lambda s, meta, c=c: (0, lax.rem(meta[ndocs], 2) * chunks + c))
        far = pl.BlockSpec((4, rows, cw), lambda s, meta, c=c: (0, 0, c))
        tail, head, even_tail, odd_head = pl.pallas_call(
            functools.partial(state_kernel, ndocs=ndocs, rows=rows, heads=heads),
            grid_spec=pltpu.PrefetchScalarGridSpec(
                num_scalar_prefetch=1, grid=(1,), in_specs=[own] * 4 + [far], out_specs=[state_spec] * 4,
            ),
            out_shape=[jax.ShapeDtypeStruct(square, f32)] * 4,
            cost_estimate=pl.CostEstimate(
                flops=8 * heads * rows * HEAD_DIM * HEAD_DIM, bytes_accessed=16 * rows * cw + 16 * heads * HEAD_DIM**2, transcendentals=0
            ),
            compiler_params=params, name="states",
        )(meta, queries, keys, values, out_grad, pair)
        tails, heads_in = [], []
        for hop in range(1, hops + 1):
            far_by = 2 * hop
            tails.append(lax.ppermute(tail, "seq", [(b, b + far_by) for b in range(seq - far_by)]))
            heads_in.append(lax.ppermute(head, "seq", [(b + far_by, b) for b in range(seq - far_by)]))
        stage.append((own, far, even_tail, odd_head, tails, heads_in))

    def grads(meta, q, k, v, g, pair, even_tail, odd_head, *rest, **sizes):
        tails, heads_in, rest = rest[:hops], rest[hops:2 * hops], rest[2 * hops:]
        grad_kernel(meta, q, k, v, g, pair, even_tail, odd_head, Pick(tails), Pick(heads_in), *rest, **sizes)

    arrived = []
    for c in range(chunks):
        own, far, even_tail, odd_head, tails, heads_in = stage[c]
        slot = pl.BlockSpec((3, part, cw), lambda s, meta: (0, 0, 0))
        outs = pl.pallas_call(
            functools.partial(grads, ndocs=ndocs, rows=rows, heads=heads, groups=groups, hops=hops),
            grid_spec=pltpu.PrefetchScalarGridSpec(
                num_scalar_prefetch=1, grid=(1,),
                in_specs=[own] * 4 + [far] + [state_spec] * (2 + 2 * hops),
                out_specs=[slot] * (2 * groups),
                scratch_shapes=[pltpu.VMEM((2, 3, rows, cw), bf16)],
            ),
            out_shape=[jax.ShapeDtypeStruct((3, part, cw), bf16)] * (2 * groups),
            cost_estimate=pl.CostEstimate(
                flops=2 * heads * (12 * rows * rows * HEAD_DIM + 12 * rows * HEAD_DIM**2),
                bytes_accessed=16 * rows * cw + 8 * (1 + hops) * heads * HEAD_DIM**2 + 12 * rows * cw, transcendentals=0,
            ),
            compiler_params=params, name="grads",
        )(meta, queries, keys, values, out_grad, pair, even_tail, odd_head, *tails, *heads_in)
        for side in range(2):
            for j in range(groups):
                out = outs[side * groups + j]
                if side or j:
                    perm = [
                        (b * groups + x, (b ^ side) * groups + (x + j) % groups) for b in range(seq) for x in range(groups)
                    ]
                    out = lax.ppermute(out, ("seq", "head"), perm)
                arrived.append(out)

    return tuple(
        pl.pallas_call(
            functools.partial(place_kernel, ndocs=ndocs, groups=groups, chunks=chunks, width=width, half=half, cw=cw),
            grid_spec=pltpu.PrefetchScalarGridSpec(
                num_scalar_prefetch=1, grid=(1,), in_specs=[anywhere] * len(arrived), out_specs=[anywhere] * 3,
                scratch_shapes=[pltpu.SemaphoreType.DMA((3 * len(arrived),))],
            ),
            out_shape=[jax.ShapeDtypeStruct((part, width * groups), bf16)] * 3,
            cost_estimate=pl.CostEstimate(flops=0, bytes_accessed=12 * part * width * groups, transcendentals=0),
            compiler_params=params, name="place",
        )(meta, *arrived)
    )


class Pick:
    def __init__(self, refs):
        self.refs = refs

    def __getitem__(self, at):
        return self.refs[at[0]][at[1]]


def solution(mesh):
    return jax.shard_map(
        shards,
        mesh=mesh,
        in_specs=(P("seq", "head"), P("seq", "head"), P("seq", "head"), P("seq", "head"), P()),
        out_specs=(P(("seq", "head"), None), P(("seq", "head"), None), P(("seq", "head"), None)),
        check_vma=False,
    )
```

time: 359 us -> 95.8 us (0.27)
  the two profiles are of different devices: /device:TPU:29 before, /device:TPU:17 now
where the time goes in v1:
time: 95.8 us; the launch traced here: 95.2 us
  waiting for transfers between devices  37.8 us (39%)
  starting transfers between devices  30.5 us (32%)
  Pallas kernels  19.2 us (20%)
  local copies, waits for them, and re-layouts  6.24 us (7%)
    ppermute x6, waiting for transfers between devices, shards(): out = lax.ppermute(out, ('seq', 'head'), perm)  17.1 us
    ppermute x4, starting transfers between devices, shards(): lax.ppermute(tail, 'seq', [(b, b + far_by) for b in range(seq - far_by)])  11.5 us
    ppermute x4, starting transfers between devices, shards(): lax.ppermute(head, 'seq', [(b + far_by, b) for b in range(seq - far_by)])  11.4 us
    ppermute x4, waiting for transfers between devices, shards(): lax.ppermute(head, 'seq', [(b + far_by, b) for b in range(seq - far_by)])  11.2 us
    pallas_call x2, Pallas kernels, shards(): pl.pallas_call(functools.partial(grads, ndocs=ndocs, rows=rows, heads=hea...  10.2 us
    ppermute x6, starting transfers between devices, shards(): out = lax.ppermute(out, ('seq', 'head'), perm)  6.85 us
    unnamed x14, local copies, waits for them, and re-layouts  6.24 us
    ppermute x4, waiting for transfers between devices, shards(): lax.ppermute(tail, 'seq', [(b, b + far_by) for b in range(seq - far_by)])  5.46 us
  transfers between devices with their start and end apart: 15, of which 7 were waited for; matrix products, arithmetic and copies ran while one was open for 0% of the time, Pallas kernels for 8%

profile of v1, /device:TPU:17, one launch (start us, length us, event | category | flops | bytes accessed | tf_op | source)
XLA Modules:
  0.0 95.2 jit_solution(7557594275323843332)
XLA Ops:
  0.6 0.7 pad_add_fusion.meta
  1.4 0.0 copy-start
  1.4 1.2 %copy-done = bf16[256,2048]{1,0:T(8,128)(2,1)S(1)} copy-done((bf16[256,2048]{1,0:T(8,128)(2,1)S(1)}, bf16[256,2048]{1,0:T(8,128)(2,1)}, u32[]{:S(2)}) %copy-start) | copy-done | bytes 1048600
  2.6 0.0 copy-start.1
  2.6 1.2 %copy-done.1 = bf16[256,2048]{1,0:T(8,128)(2,1)S(1)} copy-done((bf16[256,2048]{1,0:T(8,128)(2,1)S(1)}, bf16[256,2048]{1,0:T(8,128)(2,1)}, u32[]{:S(2)}) %copy-start.1) | copy-done | bytes 1048600
  3.8 0.0 copy-start.2
  3.8 1.2 %copy-done.2 = bf16[256,2048]{1,0:T(8,128)(2,1)S(1)} copy-done((bf16[256,2048]{1,0:T(8,128)(2,1)S(1)}, bf16[256,2048]{1,0:T(8,128)(2,1)}, u32[]{:S(2)}) %copy-start.2) | copy-done | bytes 1048600
  5.0 0.0 copy-start.4
  5.0 1.2 %copy-done.4 = bf16[256,2048]{1,0:T(8,128)(2,1)S(1)} copy-done((bf16[256,2048]{1,0:T(8,128)(2,1)S(1)}, bf16[256,2048]{1,0:T(8,128)(2,1)}, u32[]{:S(2)}) %copy-start.4) | copy-done | bytes 1048600
  6.3 1.9 %pack.1 = bf16[4,256,1024]{2,1,0:T(8,128)(2,1)} custom-call(s32[10]{0:T(128)S(1)} %pad_add_fusion.meta, bf16[256,2048]{1,0:T(8,128)(2,1)S(1)} %copy-done, bf16[256,2048]{1,0:T(8,128)(2,1)S(1)} %copy-done.1, bf16[256,2048]{1,0:T(8,128)(2,1)S(1)} %copy-done.2, bf16[256,2048]{1,0:T(8,128)(2,1)S(1)} %copy-done.4), custom_call_target="tpu_custom_call" | custom-call | bytes 4194304 | tf_op jit(solution)/shard_map/pack/pallas_call | solution.py:200
  8.2 0.7 collective-permute-start
  8.9 4.0 %collective-permute-done.pair = bf16[4,256,1024]{2,1,0:T(8,128)(2,1)S(1)} collective-permute-done((bf16[4,256,1024]{2,1,0:T(8,128)(2,1)}, bf16[4,256,1024]{2,1,0:T(8,128)(2,1)S(1)}, u32[]{:S(2)}, u32[]{:S(2)}) %collective-permute-start) | collective-permute-done | bytes 2097184 | tf_op jit(solution)/shard_map/ppermute | solution.py:210
  12.9 0.0 copy-start.6
  12.9 1.3 %copy-done.6 = bf16[4,256,1024]{2,1,0:T(8,128)(2,1)} copy-done((bf16[4,256,1024]{2,1,0:T(8,128)(2,1)}, bf16[4,256,1024]{2,1,0:T(8,128)(2,1)S(1)}, u32[]{:S(2)}) %copy-start.6) | copy-done | bytes 2097176
  14.3 2.3 %states.3 = (f32[4,128,128]{2,1,0:T(8,128)S(1)}, f32[4,128,128]{2,1,0:T(8,128)S(1)}, f32[4,128,128]{2,1,0:T(8,128)S(1)}, f32[4,128,128]{2,1,0:T(8,128)S(1)}) custom-call(s32[10]{0:T(128)S(1)} %pad_add_fusion.meta, bf16[256,2048]{1,0:T(8,128)(2,1)S(1)} %copy-done, bf16[256,2048]{1,0:T(8,128)(2,1)S(1)} %copy-done.1, bf16[256,2048]{1,0:T(8,128)(2,1)S(1)} %copy-done.2, ...), custom_call_target="tpu_custom_call" | custom-call | flops 134217728 | bytes 3145728 | tf_op jit(solution)/shard_map/states/pallas_call | solution.py:219
  16.6 3.2 %collective-permute-start.9 = (f32[4,128,128]{2,1,0:T(8,128)S(1)}, f32[4,128,128]{2,1,0:T(8,128)S(1)}, u32[]{:S(2)}, u32[]{:S(2)}) collective-permute-start(f32[4,128,128]{2,1,0:T(8,128)S(1)} %get-tuple-element.29), channel_id=1, source_target_pairs={{0,8},{2,10},{4,12},{6,14},{8,16},{10,18},{12,20},{14,22},{16,24},... | collective-permute-start | bytes 786440 | tf_op jit(solution)/shard_map/ppermute | solution.py:233
  19.8 3.1 %collective-permute-start.8 = (f32[4,128,128]{2,1,0:T(8,128)S(1)}, f32[4,128,128]{2,1,0:T(8,128)S(1)}, u32[]{:S(2)}, u32[]{:S(2)}) collective-permute-start(f32[4,128,128]{2,1,0:T(8,128)S(1)} %get-tuple-element.29), channel_id=1, source_target_pairs={{0,4},{2,6},{4,8},{6,10},{8,12},{10,14},{12,16},{14,18},{16,20},{1... | collective-permute-start | bytes 786440 | tf_op jit(solution)/shard_map/ppermute | solution.py:233
  23.0 2.1 %collective-permute-start.11 = (f32[4,128,128]{2,1,0:T(8,128)S(1)}, f32[4,128,128]{2,1,0:T(8,128)S(1)}, u32[]{:S(2)}, u32[]{:S(2)}) collective-permute-start(f32[4,128,128]{2,1,0:T(8,128)S(1)} %get-tuple-element.30), channel_id=1, source_target_pairs={{8,0},{10,2},{12,4},{14,6},{16,8},{18,10},{20,12},{22,14},{24,16},... | collective-permute-start | bytes 786440 | tf_op jit(solution)/shard_map/ppermute | solution.py:234
  25.0 3.0 %collective-permute-start.10 = (f32[4,128,128]{2,1,0:T(8,128)S(1)}, f32[4,128,128]{2,1,0:T(8,128)S(1)}, u32[]{:S(2)}, u32[]{:S(2)}) collective-permute-start(f32[4,128,128]{2,1,0:T(8,128)S(1)} %get-tuple-element.30), channel_id=1, source_target_pairs={{4,0},{6,2},{8,4},{10,6},{12,8},{14,10},{16,12},{18,14},{20,16},{2... | collective-permute-start | bytes 786440 | tf_op jit(solution)/shard_map/ppermute | solution.py:234
  28.1 0.0 collective-permute-done.9.rest_1_
  28.1 4.5 %collective-permute-done.8.rest_0_ = f32[4,128,128]{2,1,0:T(8,128)S(1)} collective-permute-done((f32[4,128,128]{2,1,0:T(8,128)S(1)}, f32[4,128,128]{2,1,0:T(8,128)S(1)}, u32[]{:S(2)}, u32[]{:S(2)}) %collective-permute-start.8) | collective-permute-done | bytes 262176 | tf_op jit(solution)/shard_map/ppermute | solution.py:233
  32.6 0.0 collective-permute-done.11.rest_3_
  32.6 6.3 %collective-permute-done.10.rest_2_ = f32[4,128,128]{2,1,0:T(8,128)S(1)} collective-permute-done((f32[4,128,128]{2,1,0:T(8,128)S(1)}, f32[4,128,128]{2,1,0:T(8,128)S(1)}, u32[]{:S(2)}, u32[]{:S(2)}) %collective-permute-start.10) | collective-permute-done | bytes 262176 | tf_op jit(solution)/shard_map/ppermute | solution.py:234
  38.9 0.0 copy-start.3
  38.9 0.0 copy-start.5
  38.9 5.2 %grads.3 = (bf16[3,128,512]{2,1,0:T(8,128)(2,1)S(1)}, bf16[3,128,512]{2,1,0:T(8,128)(2,1)S(1)}, bf16[3,128,512]{2,1,0:T(8,128)(2,1)S(1)}, bf16[3,128,512]{2,1,0:T(8,128)(2,1)S(1)}) custom-call(s32[10]{0:T(128)S(1)} %pad_add_fusion.meta, bf16[256,2048]{1,0:T(8,128)(2,1)S(1)} %copy-done, bf16[256,2048]{1,0:T(8,128)(2,1)S(1)} %copy-done.1, ...), custom_call_target="tpu_custom_call" | custom-call | flops 1207959552 | bytes 5242880 | tf_op jit(solution)/shard_map/grads/pallas_call | solution.py:245
  44.1 1.3 %collective-permute-start.12 = (bf16[3,128,512]{2,1,0:T(8,128)(2,1)S(1)}, bf16[3,128,512]{2,1,0:T(8,128)(2,1)S(1)}, u32[]{:S(2)}, u32[]{:S(2)}) collective-permute-start(bf16[3,128,512]{2,1,0:T(8,128)(2,1)S(1)} %get-tuple-element.32), channel_id=1, source_target_pairs={{0,1},{1,0},{2,3},{3,2},{4,5},{5,4},{6,7},{7,6},{8,9},{9,8},{10,11... | collective-permute-start | bytes 1179656 | tf_op jit(solution)/shard_map/ppermute | solution.py:267
  45.3 0.0 copy-done.3
  45.4 0.0 copy-done.5
  45.4 2.3 %states.2 = (f32[4,128,128]{2,1,0:T(8,128)S(1)}, f32[4,128,128]{2,1,0:T(8,128)S(1)}, f32[4,128,128]{2,1,0:T(8,128)S(1)}, f32[4,128,128]{2,1,0:T(8,128)S(1)}) custom-call(s32[10]{0:T(128)S(1)} %pad_add_fusion.meta, bf16[256,2048]{1,0:T(8,128)(2,1)S(1)} %copy-done, bf16[256,2048]{1,0:T(8,128)(2,1)S(1)} %copy-done.1, bf16[256,2048]{1,0:T(8,128)(2,1)S(1)} %copy-done.3, ...), custom_call_target="tpu_custom_call" | custom-call | flops 134217728 | bytes 3145728 | tf_op jit(solution)/shard_map/states/pallas_call | solution.py:219
  47.7 3.2 %collective-permute-start.2 = (f32[4,128,128]{2,1,0:T(8,128)S(1)}, f32[4,128,128]{2,1,0:T(8,128)S(1)}, u32[]{:S(2)}, u32[]{:S(2)}) collective-permute-start(f32[4,128,128]{2,1,0:T(8,128)S(1)} %get-tuple-element.21), channel_id=1, source_target_pairs={{0,8},{2,10},{4,12},{6,14},{8,16},{10,18},{12,20},{14,22},{16,24},... | collective-permute-start | bytes 786440 | tf_op jit(solution)/shard_map/ppermute | solution.py:233
  50.9 1.9 %collective-permute-start.1 = (f32[4,128,128]{2,1,0:T(8,128)S(1)}, f32[4,128,128]{2,1,0:T(8,128)S(1)}, u32[]{:S(2)}, u32[]{:S(2)}) collective-permute-start(f32[4,128,128]{2,1,0:T(8,128)S(1)} %get-tuple-element.21), channel_id=1, source_target_pairs={{0,4},{2,6},{4,8},{6,10},{8,12},{10,14},{12,16},{14,18},{16,20},{1... | collective-permute-start | bytes 786440 | tf_op jit(solution)/shard_map/ppermute | solution.py:233
  52.8 2.1 %collective-permute-start.4 = (f32[4,128,128]{2,1,0:T(8,128)S(1)}, f32[4,128,128]{2,1,0:T(8,128)S(1)}, u32[]{:S(2)}, u32[]{:S(2)}) collective-permute-start(f32[4,128,128]{2,1,0:T(8,128)S(1)} %get-tuple-element.22), channel_id=1, source_target_pairs={{8,0},{10,2},{12,4},{14,6},{16,8},{18,10},{20,12},{22,14},{24,16},... | collective-permute-start | bytes 786440 | tf_op jit(solution)/shard_map/ppermute | solution.py:234
  54.9 4.3 %collective-permute-start.3 = (f32[4,128,128]{2,1,0:T(8,128)S(1)}, f32[4,128,128]{2,1,0:T(8,128)S(1)}, u32[]{:S(2)}, u32[]{:S(2)}) collective-permute-start(f32[4,128,128]{2,1,0:T(8,128)S(1)} %get-tuple-element.22), channel_id=1, source_target_pairs={{4,0},{6,2},{8,4},{10,6},{12,8},{14,10},{16,12},{18,14},{20,16},{2... | collective-permute-start | bytes 786440 | tf_op jit(solution)/shard_map/ppermute | solution.py:234
  59.2 0.0 collective-permute-done.2.rest_1_
  59.2 2.0 %collective-permute-start.13 = (bf16[3,128,512]{2,1,0:T(8,128)(2,1)S(1)}, bf16[3,128,512]{2,1,0:T(8,128)(2,1)S(1)}, u32[]{:S(2)}, u32[]{:S(2)}) collective-permute-start(bf16[3,128,512]{2,1,0:T(8,128)(2,1)S(1)} %get-tuple-element.33), channel_id=1, source_target_pairs={{0,2},{1,3},{2,0},{3,1},{4,6},{5,7},{6,4},{7,5},{8,10},{9,11},{10,... | collective-permute-start | bytes 1179656 | tf_op jit(solution)/shard_map/ppermute | solution.py:267
  61.1 0.9 collective-permute-done.1.rest_0_
  62.1 1.4 %collective-permute-start.14 = (bf16[3,128,512]{2,1,0:T(8,128)(2,1)S(1)}, bf16[3,128,512]{2,1,0:T(8,128)(2,1)S(1)}, u32[]{:S(2)}, u32[]{:S(2)}) collective-permute-start(bf16[3,128,512]{2,1,0:T(8,128)(2,1)S(1)} %get-tuple-element.34), channel_id=1, source_target_pairs={{0,3},{1,2},{2,1},{3,0},{4,7},{5,6},{6,5},{7,4},{8,11},{9,10},{10,... | collective-permute-start | bytes 1179656 | tf_op jit(solution)/shard_map/ppermute | solution.py:267
  63.5 0.0 collective-permute-done.4.rest_3_
  63.5 4.9 %collective-permute-done.3.rest_2_ = f32[4,128,128]{2,1,0:T(8,128)S(1)} collective-permute-done((f32[4,128,128]{2,1,0:T(8,128)S(1)}, f32[4,128,128]{2,1,0:T(8,128)S(1)}, u32[]{:S(2)}, u32[]{:S(2)}) %collective-permute-start.3) | collective-permute-done | bytes 262176 | tf_op jit(solution)/shard_map/ppermute | solution.py:234
  68.4 5.1 %grads.2 = (bf16[3,128,512]{2,1,0:T(8,128)(2,1)S(1)}, bf16[3,128,512]{2,1,0:T(8,128)(2,1)S(1)}, bf16[3,128,512]{2,1,0:T(8,128)(2,1)S(1)}, bf16[3,128,512]{2,1,0:T(8,128)(2,1)S(1)}) custom-call(s32[10]{0:T(128)S(1)} %pad_add_fusion.meta, bf16[256,2048]{1,0:T(8,128)(2,1)S(1)} %copy-done, bf16[256,2048]{1,0:T(8,128)(2,1)S(1)} %copy-done.1, ...), custom_call_target="tpu_custom_call" | custom-call | flops 1207959552 | bytes 5242880 | tf_op jit(solution)/shard_map/grads/pallas_call | solution.py:245
  73.5 0.3 collective-permute-start.5
  73.8 0.8 collective-permute-start.6
  74.6 0.0 collective-permute-done.12.refs_5_
  74.6 1.1 %collective-permute-start.7 = (bf16[3,128,512]{2,1,0:T(8,128)(2,1)S(1)}, bf16[3,128,512]{2,1,0:T(8,128)(2,1)S(1)}, u32[]{:S(2)}, u32[]{:S(2)}) collective-permute-start(bf16[3,128,512]{2,1,0:T(8,128)(2,1)S(1)} %get-tuple-element.26), channel_id=1, source_target_pairs={{0,3},{1,2},{2,1},{3,0},{4,7},{5,6},{6,5},{7,4},{8,11},{9,10},{10,... | collective-permute-start | bytes 1179656 | tf_op jit(solution)/shard_map/ppermute | solution.py:267
  75.7 0.0 collective-permute-done.13.refs_6_
  75.7 0.0 collective-permute-done.14.refs_7_
  75.7 8.1 %collective-permute-done.5.refs_1_ = bf16[3,128,512]{2,1,0:T(8,128)(2,1)S(1)} collective-permute-done((bf16[3,128,512]{2,1,0:T(8,128)(2,1)S(1)}, bf16[3,128,512]{2,1,0:T(8,128)(2,1)S(1)}, u32[]{:S(2)}, u32[]{:S(2)}) %collective-permute-start.5) | collective-permute-done | bytes 393248 | tf_op jit(solution)/shard_map/ppermute | solution.py:267
  83.7 0.0 collective-permute-done.6.refs_2_
  83.7 9.1 %collective-permute-done.7.refs_3_ = bf16[3,128,512]{2,1,0:T(8,128)(2,1)S(1)} collective-permute-done((bf16[3,128,512]{2,1,0:T(8,128)(2,1)S(1)}, bf16[3,128,512]{2,1,0:T(8,128)(2,1)S(1)}, u32[]{:S(2)}, u32[]{:S(2)}) %collective-permute-start.7) | collective-permute-done | bytes 393248 | tf_op jit(solution)/shard_map/ppermute | solution.py:267
  92.8 2.4 %place.1 = (bf16[128,4096]{1,0:T(8,128)(2,1)}, bf16[128,4096]{1,0:T(8,128)(2,1)}, bf16[128,4096]{1,0:T(8,128)(2,1)}) custom-call(s32[10]{0:T(128)S(1)} %pad_add_fusion.meta, bf16[3,128,512]{2,1,0:T(8,128)(2,1)S(1)} %get-tuple-element.23.refs_0_, bf16[3,128,512]{2,1,0:T(8,128)(2,1)S(1)} %collective-permute-done.5.refs_1_, ...), custom_call_target="tpu_custom_call" | custom-call | bytes 6291456 | tf_op jit(solution)/shard_map/place/pallas_call | solution.py:271
Async XLA Ops:
  1.4 1.2 %copy-start = (bf16[256,2048]{1,0:T(8,128)(2,1)S(1)}, bf16[256,2048]{1,0:T(8,128)(2,1)}, u32[]{:S(2)}) copy-start(bf16[256,2048]{1,0:T(8,128)(2,1)} %q.9) | copy-start | bytes 3145732
  2.6 1.2 %copy-start.1 = (bf16[256,2048]{1,0:T(8,128)(2,1)S(1)}, bf16[256,2048]{1,0:T(8,128)(2,1)}, u32[]{:S(2)}) copy-start(bf16[256,2048]{1,0:T(8,128)(2,1)} %k.9) | copy-start | bytes 3145732
  3.8 1.2 %copy-start.2 = (bf16[256,2048]{1,0:T(8,128)(2,1)S(1)}, bf16[256,2048]{1,0:T(8,128)(2,1)}, u32[]{:S(2)}) copy-start(bf16[256,2048]{1,0:T(8,128)(2,1)} %v.9) | copy-start | bytes 3145732
  5.0 1.2 %copy-start.4 = (bf16[256,2048]{1,0:T(8,128)(2,1)S(1)}, bf16[256,2048]{1,0:T(8,128)(2,1)}, u32[]{:S(2)}) copy-start(bf16[256,2048]{1,0:T(8,128)(2,1)} %g.9) | copy-start | bytes 3145732
  8.2 4.7 %collective-permute-start = (bf16[4,256,1024]{2,1,0:T(8,128)(2,1)}, bf16[4,256,1024]{2,1,0:T(8,128)(2,1)S(1)}, u32[]{:S(2)}, u32[]{:S(2)}) collective-permute-start(bf16[4,256,1024]{2,1,0:T(8,128)(2,1)} %pack.1), channel_id=1, source_target_pairs={{0,2},{2,0},{4,6},{6,4},{8,10},{10,8},{12,14},{14,12},{16,18},{18,... | collective-permute-start | bytes 6291464 | tf_op jit(solution)/shard_map/ppermute | solution.py:210
  12.9 1.3 %copy-start.6 = (bf16[4,256,1024]{2,1,0:T(8,128)(2,1)}, bf16[4,256,1024]{2,1,0:T(8,128)(2,1)S(1)}, u32[]{:S(2)}) copy-start(bf16[4,256,1024]{2,1,0:T(8,128)(2,1)S(1)} %collective-permute-done.pair) | copy-start | bytes 6291460
  16.6 11.5 %collective-permute-start.9 = (f32[4,128,128]{2,1,0:T(8,128)S(1)}, f32[4,128,128]{2,1,0:T(8,128)S(1)}, u32[]{:S(2)}, u32[]{:S(2)}) collective-permute-start(f32[4,128,128]{2,1,0:T(8,128)S(1)} %get-tuple-element.29), channel_id=1, source_target_pairs={{0,8},{2,10},{4,12},{6,14},{8,16},{10,18},{12,20},{14,22},{16,24},... | collective-permute-start | bytes 786440 | tf_op jit(solution)/shard_map/ppermute | solution.py:233
  19.8 12.8 %collective-permute-start.8 = (f32[4,128,128]{2,1,0:T(8,128)S(1)}, f32[4,128,128]{2,1,0:T(8,128)S(1)}, u32[]{:S(2)}, u32[]{:S(2)}) collective-permute-start(f32[4,128,128]{2,1,0:T(8,128)S(1)} %get-tuple-element.29), channel_id=1, source_target_pairs={{0,4},{2,6},{4,8},{6,10},{8,12},{10,14},{12,16},{14,18},{16,20},{1... | collective-permute-start | bytes 786440 | tf_op jit(solution)/shard_map/ppermute | solution.py:233
  23.0 9.7 %collective-permute-start.11 = (f32[4,128,128]{2,1,0:T(8,128)S(1)}, f32[4,128,128]{2,1,0:T(8,128)S(1)}, u32[]{:S(2)}, u32[]{:S(2)}) collective-permute-start(f32[4,128,128]{2,1,0:T(8,128)S(1)} %get-tuple-element.30), channel_id=1, source_target_pairs={{8,0},{10,2},{12,4},{14,6},{16,8},{18,10},{20,12},{22,14},{24,16},... | collective-permute-start | bytes 786440 | tf_op jit(solution)/shard_map/ppermute | solution.py:234
  25.0 13.9 %collective-permute-start.10 = (f32[4,128,128]{2,1,0:T(8,128)S(1)}, f32[4,128,128]{2,1,0:T(8,128)S(1)}, u32[]{:S(2)}, u32[]{:S(2)}) collective-permute-start(f32[4,128,128]{2,1,0:T(8,128)S(1)} %get-tuple-element.30), channel_id=1, source_target_pairs={{4,0},{6,2},{8,4},{10,6},{12,8},{14,10},{16,12},{18,14},{20,16},{2... | collective-permute-start | bytes 786440 | tf_op jit(solution)/shard_map/ppermute | solution.py:234
  38.9 6.4 %copy-start.3 = (bf16[256,2048]{1,0:T(8,128)(2,1)S(1)}, bf16[256,2048]{1,0:T(8,128)(2,1)}, u32[]{:S(2)}) copy-start(bf16[256,2048]{1,0:T(8,128)(2,1)} %v.9) | copy-start | bytes 3145732
  38.9 6.4 %copy-start.5 = (bf16[256,2048]{1,0:T(8,128)(2,1)S(1)}, bf16[256,2048]{1,0:T(8,128)(2,1)}, u32[]{:S(2)}) copy-start(bf16[256,2048]{1,0:T(8,128)(2,1)} %g.9) | copy-start | bytes 3145732
  44.1 30.5 %collective-permute-start.12 = (bf16[3,128,512]{2,1,0:T(8,128)(2,1)S(1)}, bf16[3,128,512]{2,1,0:T(8,128)(2,1)S(1)}, u32[]{:S(2)}, u32[]{:S(2)}) collective-permute-start(bf16[3,128,512]{2,1,0:T(8,128)(2,1)S(1)} %get-tuple-element.32), channel_id=1, source_target_pairs={{0,1},{1,0},{2,3},{3,2},{4,5},{5,4},{6,7},{7,6},{8,9},{9,8},{10,11... | collective-permute-start | bytes 1179656 | tf_op jit(solution)/shard_map/ppermute | solution.py:267
  47.7 11.5 %collective-permute-start.2 = (f32[4,128,128]{2,1,0:T(8,128)S(1)}, f32[4,128,128]{2,1,0:T(8,128)S(1)}, u32[]{:S(2)}, u32[]{:S(2)}) collective-permute-start(f32[4,128,128]{2,1,0:T(8,128)S(1)} %get-tuple-element.21), channel_id=1, source_target_pairs={{0,8},{2,10},{4,12},{6,14},{8,16},{10,18},{12,20},{14,22},{16,24},... | collective-permute-start | bytes 786440 | tf_op jit(solution)/shard_map/ppermute | solution.py:233
  50.9 11.2 %collective-permute-start.1 = (f32[4,128,128]{2,1,0:T(8,128)S(1)}, f32[4,128,128]{2,1,0:T(8,128)S(1)}, u32[]{:S(2)}, u32[]{:S(2)}) collective-permute-start(f32[4,128,128]{2,1,0:T(8,128)S(1)} %get-tuple-element.21), channel_id=1, source_target_pairs={{0,4},{2,6},{4,8},{6,10},{8,12},{10,14},{12,16},{14,18},{16,20},{1... | collective-permute-start | bytes 786440 | tf_op jit(solution)/shard_map/ppermute | solution.py:233
  52.8 10.7 %collective-permute-start.4 = (f32[4,128,128]{2,1,0:T(8,128)S(1)}, f32[4,128,128]{2,1,0:T(8,128)S(1)}, u32[]{:S(2)}, u32[]{:S(2)}) collective-permute-start(f32[4,128,128]{2,1,0:T(8,128)S(1)} %get-tuple-element.22), channel_id=1, source_target_pairs={{8,0},{10,2},{12,4},{14,6},{16,8},{18,10},{20,12},{22,14},{24,16},... | collective-permute-start | bytes 786440 | tf_op jit(solution)/shard_map/ppermute | solution.py:234
  54.9 13.5 %collective-permute-start.3 = (f32[4,128,128]{2,1,0:T(8,128)S(1)}, f32[4,128,128]{2,1,0:T(8,128)S(1)}, u32[]{:S(2)}, u32[]{:S(2)}) collective-permute-start(f32[4,128,128]{2,1,0:T(8,128)S(1)} %get-tuple-element.22), channel_id=1, source_target_pairs={{4,0},{6,2},{8,4},{10,6},{12,8},{14,10},{16,12},{18,14},{20,16},{2... | collective-permute-start | bytes 786440 | tf_op jit(solution)/shard_map/ppermute | solution.py:234
  59.2 16.5 %collective-permute-start.13 = (bf16[3,128,512]{2,1,0:T(8,128)(2,1)S(1)}, bf16[3,128,512]{2,1,0:T(8,128)(2,1)S(1)}, u32[]{:S(2)}, u32[]{:S(2)}) collective-permute-start(bf16[3,128,512]{2,1,0:T(8,128)(2,1)S(1)} %get-tuple-element.33), channel_id=1, source_target_pairs={{0,2},{1,3},{2,0},{3,1},{4,6},{5,7},{6,4},{7,5},{8,10},{9,11},{10,... | collective-permute-start | bytes 1179656 | tf_op jit(solution)/shard_map/ppermute | solution.py:267
  62.1 13.6 %collective-permute-start.14 = (bf16[3,128,512]{2,1,0:T(8,128)(2,1)S(1)}, bf16[3,128,512]{2,1,0:T(8,128)(2,1)S(1)}, u32[]{:S(2)}, u32[]{:S(2)}) collective-permute-start(bf16[3,128,512]{2,1,0:T(8,128)(2,1)S(1)} %get-tuple-element.34), channel_id=1, source_target_pairs={{0,3},{1,2},{2,1},{3,0},{4,7},{5,6},{6,5},{7,4},{8,11},{9,10},{10,... | collective-permute-start | bytes 1179656 | tf_op jit(solution)/shard_map/ppermute | solution.py:267
  73.5 10.3 %collective-permute-start.5 = (bf16[3,128,512]{2,1,0:T(8,128)(2,1)S(1)}, bf16[3,128,512]{2,1,0:T(8,128)(2,1)S(1)}, u32[]{:S(2)}, u32[]{:S(2)}) collective-permute-start(bf16[3,128,512]{2,1,0:T(8,128)(2,1)S(1)} %get-tuple-element.24), channel_id=1, source_target_pairs={{0,1},{1,0},{2,3},{3,2},{4,5},{5,4},{6,7},{7,6},{8,9},{9,8},{10,11... | collective-permute-start | bytes 1179656 | tf_op jit(solution)/shard_map/ppermute | solution.py:267
  73.8 9.9 %collective-permute-start.6 = (bf16[3,128,512]{2,1,0:T(8,128)(2,1)S(1)}, bf16[3,128,512]{2,1,0:T(8,128)(2,1)S(1)}, u32[]{:S(2)}, u32[]{:S(2)}) collective-permute-start(bf16[3,128,512]{2,1,0:T(8,128)(2,1)S(1)} %get-tuple-element.25), channel_id=1, source_target_pairs={{0,2},{1,3},{2,0},{3,1},{4,6},{5,7},{6,4},{7,5},{8,10},{9,11},{10,... | collective-permute-start | bytes 1179656 | tf_op jit(solution)/shard_map/ppermute | solution.py:267
  74.6 18.2 %collective-permute-start.7 = (bf16[3,128,512]{2,1,0:T(8,128)(2,1)S(1)}, bf16[3,128,512]{2,1,0:T(8,128)(2,1)S(1)}, u32[]{:S(2)}, u32[]{:S(2)}) collective-permute-start(bf16[3,128,512]{2,1,0:T(8,128)(2,1)S(1)} %get-tuple-element.26), channel_id=1, source_target_pairs={{0,3},{1,2},{2,1},{3,0},{4,7},{5,6},{6,5},{7,4},{8,11},{9,10},{10,... | collective-permute-start | bytes 1179656 | tf_op jit(solution)/shard_map/ppermute | solution.py:267

commit v2 on v0

v2 whole, which is shorter than its diff:
```python
import functools

import jax
import jax.numpy as jnp
from jax import lax
from jax.experimental import pallas as pl
from jax.experimental.pallas import tpu as pltpu
from jax.sharding import PartitionSpec as P

HEAD_DIM = 128
MOST = 1024
CUTS = (8, 8)
VMEM_LIMIT = 32 * 1024 * 1024
FIRST_LIMIT = 60 * 1024 * 1024
NT = (((1,), (1,)), ((), ()))
TN = (((0,), (0,)), ((), ()))
NN = (((1,), (0,)), ((), ()))


def dot(a, b, dims):
    return lax.dot_general(a, b, dims, preferred_element_type=jnp.float32)


def doc_at(meta, ndocs, position):
    start, begin, end = jnp.int32(0), jnp.int32(0), jnp.int32(0)
    for i in range(ndocs):
        stop = start + meta[i]
        begin = jnp.where(start <= position, start, begin)
        end = jnp.where(start <= position, stop, end)
        start = stop
    return begin, end


def block_range(meta, ndocs, base, rows):
    begin0, end0 = doc_at(meta, ndocs, base)
    begin1, end1 = doc_at(meta, ndocs, base + rows - 1)
    first = jnp.where(begin0 < base, end0, base) - base
    return begin0, end0, begin1, end1, first, begin1 - base


def goes_up(place, hop):
    return lax.rem(lax.div(lax.div(place, 2), hop), 2) == 0


def state_kernel(lengths, q, k, v, g, *rest, ndocs, rows, heads):
    kept, sent = rest[-2:]
    place = lax.axis_index("seq")
    first_core = lax.rem(place, 2) == 0
    _, _, _, _, first, last = block_range(lengths, ndocs, place * rows, rows)
    order = lax.broadcasted_iota(jnp.int32, (rows, HEAD_DIM), 0)
    first_rows, last_rows = order < first, order >= last
    zero = jnp.zeros((), q.dtype)

    def one(h):
        cols = slice(h * HEAD_DIM, (h + 1) * HEAD_DIM)
        tail = dot(jnp.where(last_rows, k[:, cols], zero), v[:, cols], TN)
        return tail, dot(jnp.where(first_rows, q[:, cols], zero), g[:, cols], TN)

    for i in range(heads // 2):
        for which, (low, high) in enumerate(zip(one(i), one(i + heads // 2))):
            kept[which, i] = jnp.where(first_core, low, high)
            sent[which, i] = jnp.where(first_core, high, low)


def pair_parts(kept, got, first_core, i):
    tail_even = jnp.where(first_core, kept[0, i], got[0, i])
    tail_odd = jnp.where(first_core, got[0, i], kept[0, i])
    head_even = jnp.where(first_core, kept[1, i], got[1, i])
    head_odd = jnp.where(first_core, got[1, i], kept[1, i])
    return tail_even, tail_odd, head_even, head_odd


def pair_kernel(lengths, kept, got, *rest, ndocs, rows, count, hops):
    sent = rest[-2 * hops:]
    place = lax.axis_index("seq")
    first_core = lax.rem(place, 2) == 0
    even = (place - lax.rem(place, 2)) * rows
    odd = even + rows
    _, even_e0 = doc_at(lengths, ndocs, even)
    odd_b1, _ = doc_at(lengths, ndocs, odd + rows - 1)
    tail_joins = jnp.where(odd_b1 < odd, 1.0, 0.0)
    head_joins = jnp.where(even_e0 > odd, 1.0, 0.0)
    ups = [goes_up(place, hop) for hop in range(1, hops + 1)]
    for i in range(count):
        tail_even, tail_odd, head_even, head_odd = pair_parts(kept, got, first_core, i)
        tail = tail_odd + tail_joins * tail_even
        head = head_even + head_joins * head_odd
        for hop in range(hops):
            sent[2 * hop][i] = jnp.where(ups[hop], tail, head)
            sent[2 * hop + 1][i] = jnp.where(ups[hop], head, tail)


def join_kernel(lengths, kept, got, *rest, ndocs, rows, count, hops):
    came, (mine, theirs) = rest[:2 * hops], rest[-2:]
    place = lax.axis_index("seq")
    first_core = lax.rem(place, 2) == 0
    even = (place - lax.rem(place, 2)) * rows
    odd = even + rows
    even_b0, _ = doc_at(lengths, ndocs, even)
    _, even_e1 = doc_at(lengths, ndocs, odd - 1)
    odd_b0, _ = doc_at(lengths, ndocs, odd)
    _, odd_e1 = doc_at(lengths, ndocs, odd + rows - 1)

    def one(flag):
        return jnp.where(flag, 1.0, 0.0)

    ups = [goes_up(place, hop) for hop in range(1, hops + 1)]
    tail_w = [one(even - hop * 2 * rows > even_b0) for hop in range(hops)]
    head_w = [one(odd + rows + hop * 2 * rows < odd_e1) for hop in range(hops)]
    state_from_tail, state_from_pair = one(odd > odd_b0), one(even > odd_b0)
    grad_from_head, grad_from_pair = one(odd < even_e1), one(odd + rows < even_e1)
    for i in range(count):
        tail_even, _, _, head_odd = pair_parts(kept, got, first_core, i)
        state_even, grad_odd = 0.0, 0.0
        for hop in range(hops):
            a, b = came[2 * hop][i], came[2 * hop + 1][i]
            state_even = state_even + tail_w[hop] * jnp.where(ups[hop], b, a)
            grad_odd = grad_odd + head_w[hop] * jnp.where(ups[hop], a, b)
        state_odd = state_from_tail * tail_even + state_from_pair * state_even
        grad_even = grad_from_head * head_odd + grad_from_pair * grad_odd
        mine[0, i] = jnp.where(first_core, state_even, state_odd)
        mine[1, i] = jnp.where(first_core, grad_even, grad_odd)
        theirs[0, i] = jnp.where(first_core, state_odd, state_even)
        theirs[1, i] = jnp.where(first_core, grad_odd, grad_even)


def split(a, axis):
    high = a.astype(jnp.bfloat16)
    return jnp.concatenate([high, (a - high.astype(jnp.float32)).astype(jnp.bfloat16)], axis=axis)


def local_kernel(lengths, q, k, v, g, *rest, ndocs, rows, heads):
    out = rest[-1]
    line = lax.broadcasted_iota(jnp.int32, (rows, rows), 0)
    across = lax.broadcasted_iota(jnp.int32, (rows, rows), 1)
    begin_line = jnp.zeros((rows, rows), jnp.int32)
    begin_across = jnp.zeros((rows, rows), jnp.int32)
    start = jnp.int32(0) - lax.axis_index("seq") * rows
    for i in range(ndocs):
        begin_line = jnp.where(line >= start, start, begin_line)
        begin_across = jnp.where(across >= start, start, begin_across)
        start = start + lengths[i]
    lower = (across <= line) & (across >= begin_line)
    upper = (line <= across) & (line >= begin_across)
    for h in range(heads):
        cols = slice(h * HEAD_DIM, (h + 1) * HEAD_DIM)
        qh, kh, vh, gh = (ref[:, cols] for ref in (q, k, v, g))
        weight_gv = jnp.where(lower, dot(gh, vh, NT), 0.0).astype(jnp.bfloat16)
        weight_vg = jnp.where(upper, dot(vh, gh, NT), 0.0).astype(jnp.bfloat16)
        weight_kq = jnp.where(upper, dot(kh, qh, NT), 0.0).astype(jnp.bfloat16)
        out[0, :, cols] = dot(weight_gv, kh, NN)
        out[1, :, cols] = dot(weight_vg, qh, NN)
        out[2, :, cols] = dot(weight_kq, gh, NN)


def carry_kernel(lengths, k, v, g, local, mine, got, *rest, ndocs, rows, heads, groups):
    outs, done = rest[-1 - groups:-1], rest[-1]
    place, column = lax.axis_index("seq"), lax.axis_index("head")
    first_core = lax.rem(place, 2) == 0
    _, _, _, _, first, last = block_range(lengths, ndocs, place * rows, rows)
    order = lax.broadcasted_iota(jnp.int32, (rows, HEAD_DIM), 0)
    first_rows, last_rows = order < first, order >= last
    count = heads // 2
    for h in range(heads):
        cols = slice(h * HEAD_DIM, (h + 1) * HEAD_DIM)
        here = first_core if h < count else jnp.logical_not(first_core)
        state, grad = (jnp.where(here, mine[which, h % count], got[which, h % count]) for which in range(2))
        kh, vh, gh = (jnp.concatenate([ref[:, cols]] * 2, axis=1) for ref in (k, v, g))
        carry_q = jnp.where(first_rows, dot(gh, split(state, 1), NT), 0.0)
        carry_k = jnp.where(last_rows, dot(vh, split(grad, 1), NT), 0.0)
        carry_v = jnp.where(last_rows, dot(kh, split(grad, 0), NN), 0.0)
        for i, carry in enumerate((carry_q, carry_k, carry_v)):
            done[i, :, cols] = (local[i, :, cols] + carry).astype(jnp.bfloat16)
    part = rows // groups
    for j in range(groups):
        at = pl.ds(pl.multiple_of(lax.rem(column + j, groups) * part, part), part)
        for i in range(3):
            outs[j][i] = done[i, at, :]


def place_kernel(*refs, groups, cuts, width):
    total = groups * len(cuts)
    parts, outs, sems = refs[:total], refs[total:total + 3], refs[total + 3]
    column = lax.axis_index("head")
    copies = []
    for c, (offset, cw) in enumerate(cuts):
        for j in range(groups):
            start = pl.multiple_of(lax.rem(column + groups - j, groups) * width + offset, 128)
            for i in range(3):
                dst = outs[i].at[:, pl.ds(start, cw)]
                copies.append(pltpu.make_async_copy(parts[c * groups + j].at[i], dst, sems.at[len(copies)]))
                copies[-1].start()
    for copy in copies:
        copy.wait()


def cuts_of(width):
    heads = width // HEAD_DIM
    sizes = CUTS if sum(CUTS) == heads else (2,) * (heads // 2)
    offsets = [sum(sizes[:c]) for c in range(len(sizes))]
    return [(o * HEAD_DIM, s * HEAD_DIM) for o, s in zip(offsets, sizes)]


def shards(queries, keys, values, out_grad, doc_lengths):
    rows, width = queries.shape
    ndocs = doc_lengths.shape[0]
    seq, groups = lax.axis_size("seq"), lax.axis_size("head")
    pairs = seq // 2
    hops = -(-MOST // (2 * rows))
    cuts = cuts_of(width)
    part = rows // groups
    anywhere = pl.BlockSpec(memory_space=pl.ANY)
    f32, bf16 = jnp.float32, jnp.bfloat16
    inputs = (queries, keys, values, out_grad)

    def whole(shape):
        return pl.BlockSpec(shape, lambda s, lengths: (0,) * len(shape))

    def call(name, kernel, args, in_specs, outs, after=(), flops=0, scratch=(), limit=VMEM_LIMIT):
        moved = sum(a.size * a.dtype.itemsize for a in outs) * 2
        return pl.pallas_call(
            kernel,
            grid_spec=pltpu.PrefetchScalarGridSpec(
                num_scalar_prefetch=1, grid=(1,), in_specs=list(in_specs) + [anywhere] * len(after),
                out_specs=[whole(a.shape) for a in outs], scratch_shapes=list(scratch),
            ),
            out_shape=outs,
            cost_estimate=pl.CostEstimate(flops=0, bytes_accessed=1024, transcendentals=0),
            compiler_params=pltpu.CompilerParams(vmem_limit_bytes=limit), name=name,
        )(doc_lengths, *args, *after)

    def swap_cores(a):
        return lax.ppermute(a, "seq", [(b, b ^ 1) for b in range(seq)])

    def swap_pairs(sent):
        came = []
        for hop in range(1, hops + 1):
            for turn in range(2):
                lower = [m for m in range(pairs - hop) if (m // hop) % 2 == turn]
                perm = [(2 * m + core, 2 * (m + hop) + core) for m in lower for core in range(2)]
                came.append(lax.ppermute(sent[2 * (hop - 1) + turn], "seq", perm + [(b, a) for a, b in perm]))
        return came

    def send_rows(outs):
        arrived = list(outs[:1])
        for j in range(1, groups):
            arrived.append(lax.ppermute(outs[j], "head", [(x, (x + j) % groups) for x in range(groups)]))
        return arrived

    class Chunk:
        def __init__(self, offset, cw):
            self.cw, self.heads = cw, cw // HEAD_DIM
            self.count = self.heads // 2
            self.own = pl.BlockSpec((rows, cw), lambda s, lengths: (0, offset // cw))
            self.square = (self.count, HEAD_DIM, HEAD_DIM)
            self.both = jax.ShapeDtypeStruct((2,) + self.square, f32)
            self.sizes = dict(ndocs=ndocs, rows=rows)

        def states(self, after=(), limit=VMEM_LIMIT):
            kernel = functools.partial(state_kernel, heads=self.heads, **self.sizes)
            flops = 4 * self.heads * rows * HEAD_DIM**2
            self.kept, sent = call("states", kernel, inputs, [self.own] * 4, [self.both] * 2, after, flops, limit=limit)
            self.got = swap_cores(sent)

        def pair_up(self, after=()):
            kernel = functools.partial(pair_kernel, count=self.count, hops=hops, **self.sizes)
            sent = call(
                "pair", kernel, (self.kept, self.got), [whole(self.both.shape)] * 2,
                [jax.ShapeDtypeStruct(self.square, f32)] * (2 * hops), after,
            )
            self.sent = sent
            self.came = swap_pairs(sent)

        def join(self, after=()):
            kernel = functools.partial(join_kernel, count=self.count, hops=hops, **self.sizes)
            specs = [whole(self.both.shape)] * 2 + [whole(self.square)] * (2 * hops)
            self.mine, theirs = call("join", kernel, (self.kept, self.got, *self.came), specs, [self.both] * 2, after)
            self.state = swap_cores(theirs)

        def local(self, after=()):
            kernel = functools.partial(local_kernel, heads=self.heads, **self.sizes)
            flops = 12 * self.heads * rows * rows * HEAD_DIM
            out = jax.ShapeDtypeStruct((3, rows, self.cw), f32)
            self.near = call("local", kernel, inputs, [self.own] * 4, [out], after, flops)[0]

        def carry(self, after=()):
            kernel = functools.partial(carry_kernel, heads=self.heads, groups=groups, **self.sizes)
            specs = [self.own] * 3 + [whole((3, rows, self.cw))] + [whole(self.both.shape)] * 2
            self.outs = call(
                "carry", kernel, (keys, values, out_grad, self.near, self.mine, self.state), specs,
                [jax.ShapeDtypeStruct((3, part, self.cw), bf16)] * groups, after,
                12 * self.heads * rows * HEAD_DIM**2, [pltpu.VMEM((3, rows, self.cw), bf16)],
            )
            self.arrived = send_rows(self.outs)

    chunks = [Chunk(*cut) for cut in cuts]
    chunks[0].states(limit=FIRST_LIMIT)
    for before, chunk in zip(chunks, chunks[1:]):
        chunk.states([before.kept])
    last = chunks[-1].kept
    chunks[0].pair_up([last])
    last = chunks[0].sent[0]
    for chunk in chunks:
        chunk.local([last])
        last = chunk.near
        chunk.join([last])
        last = chunk.mine
        behind = chunks.index(chunk) + 1
        if behind < len(chunks):
            chunks[behind].pair_up([last])
        chunk.carry()
        last = chunk.outs[0]

    parts = [a for chunk in chunks for a in chunk.arrived]
    return tuple(
        pl.pallas_call(
            functools.partial(place_kernel, groups=groups, cuts=cuts, width=width),
            grid_spec=pl.GridSpec(
                grid=(1,), in_specs=[anywhere] * len(parts), out_specs=[anywhere] * 3,
                scratch_shapes=[pltpu.SemaphoreType.DMA((3 * len(parts),))],
            ),
            out_shape=[jax.ShapeDtypeStruct((part, width * groups), bf16)] * 3,
            cost_estimate=pl.CostEstimate(flops=0, bytes_accessed=12 * part * width * groups, transcendentals=0),
            compiler_params=pltpu.CompilerParams(vmem_limit_bytes=VMEM_LIMIT), name="place",
        )(*parts)
    )


def solution(mesh):
    return jax.shard_map(
        shards,
        mesh=mesh,
        in_specs=(P("seq", "head"), P("seq", "head"), P("seq", "head"), P("seq", "head"), P()),
        out_specs=(P(("seq", "head"), None), P(("seq", "head"), None), P(("seq", "head"), None)),
        check_vma=False,
    )
```

time: 359 us -> 86.5 us (0.24)
  the two profiles are of different devices: /device:TPU:29 before, /device:TPU:0 now
where the time goes in v2:
time: 86.5 us; the launch traced here: 86.3 us
  waiting for transfers between devices  44.9 us (52%)
  Pallas kernels  19.5 us (23%)
  starting transfers between devices  18.8 us (22%)
  local copies, waits for them, and re-layouts  2.28 us (3%)
    ppermute x2, waiting for transfers between devices, send_rows(): lax.ppermute(outs[j], 'head', [(x, (x + j) % groups) for x in range(group...  31.3 us
    pallas_call x10, Pallas kernels, call(): pl.pallas_call(kernel, grid_spec=pltpu.PrefetchScalarGridSpec(num_scalar_...  17.7 us
    ppermute x8, starting transfers between devices, swap_pairs(): lax.ppermute(sent[2 * (hop - 1) + turn], 'seq', perm + [(b, a) for a, b i...  14.9 us
    ppermute x8, waiting for transfers between devices, swap_pairs(): lax.ppermute(sent[2 * (hop - 1) + turn], 'seq', perm + [(b, a) for a, b i...  13.2 us
    ppermute x2, starting transfers between devices, send_rows(): lax.ppermute(outs[j], 'head', [(x, (x + j) % groups) for x in range(group...  3.11 us
    unnamed x14, local copies, waits for them, and re-layouts  2.28 us
    pallas_call x1, Pallas kernels, shards(): pl.pallas_call(functools.partial(place_kernel, groups=groups, cuts=cuts,...  1.75 us
  transfers between devices with their start and end apart: 14, of which 6 were waited for; matrix products, arithmetic and copies ran while one was open for 0% of the time, Pallas kernels for 15%

profile of v2, /device:TPU:0, one launch (start us, length us, event | category | flops | bytes accessed | tf_op | source)
XLA Modules:
  0.0 86.3 jit_solution(6537138971724030520)
XLA Ops:
  0.6 0.0 copy-start.6
  0.6 0.0 copy-start.2
  0.7 0.0 copy-start.1
  0.7 0.0 copy-start
  0.7 4.0 %states.2 = (f32[2,4,128,128]{3,2,1,0:T(8,128)}, f32[2,4,128,128]{3,2,1,0:T(8,128)}) custom-call(s32[8]{0:T(128)} %lengths.19, bf16[256,2048]{1,0:T(8,128)(2,1)} %q.7, bf16[256,2048]{1,0:T(8,128)(2,1)} %k.11, bf16[256,2048]{1,0:T(8,128)(2,1)} %v.11, bf16[256,2048]{1,0:T(8,128)(2,1)} %g.11), custom_call_target="tpu_custom_call" | custom-call | bytes 1024 | tf_op jit(solution)/shard_map/states/pallas_call | solution.py:221
  4.6 0.5 collective-permute-start
  5.1 0.0 copy-done.6
  5.1 0.0 copy-done.2
  5.1 0.0 copy-done.1
  5.1 0.0 copy-done
  5.1 0.0 copy-start.3
  5.1 1.2 %copy-done.3 = bf16[256,2048]{1,0:T(8,128)(2,1)S(1)} copy-done((bf16[256,2048]{1,0:T(8,128)(2,1)S(1)}, bf16[256,2048]{1,0:T(8,128)(2,1)}, u32[]{:S(2)}) %copy-start.3) | copy-done | bytes 1048600
  6.3 0.0 copy-start.5
  6.3 1.0 %copy-done.5 = f32[2,4,128,128]{3,2,1,0:T(8,128)S(1)} copy-done((f32[2,4,128,128]{3,2,1,0:T(8,128)S(1)}, f32[2,4,128,128]{3,2,1,0:T(8,128)}, u32[]{:S(2)}) %copy-start.5) | copy-done | bytes 524312
  7.4 0.0 copy-start.4
  7.4 1.3 %states.3 = (f32[2,4,128,128]{3,2,1,0:T(8,128)S(1)}, f32[2,4,128,128]{3,2,1,0:T(8,128)S(1)}) custom-call(s32[8]{0:T(128)S(1)} %copy-done.6, bf16[256,2048]{1,0:T(8,128)(2,1)S(1)} %copy-done.3, bf16[256,2048]{1,0:T(8,128)(2,1)S(1)} %copy-done, bf16[256,2048]{1,0:T(8,128)(2,1)S(1)} %copy-done.1, bf16[256,2048]{1,0:T(8,128)(2,1)S(1)} %copy-done.2, ...), custom_call_target="tpu_custom_call" | custom-call | bytes 1024 | tf_op jit(solution)/shard_map/states/pallas_call | solution.py:221
  8.7 0.1 collective-permute-start.7
  8.8 0.0 collective-permute-done.got
  8.8 0.7 pair.2
  9.5 0.7 collective-permute-start.2
  10.2 5.7 %collective-permute-start.3 = (f32[4,128,128]{2,1,0:T(8,128)S(1)}, f32[4,128,128]{2,1,0:T(8,128)S(1)}, u32[]{:S(2)}, u32[]{:S(2)}) collective-permute-start(f32[4,128,128]{2,1,0:T(8,128)S(1)} %get-tuple-element.28), channel_id=1, source_target_pairs={{0,8},{2,10},{4,12},{6,14},{16,24},{18,26},{20,28},{22,30},{8,0},{... | collective-permute-start | bytes 786440 | tf_op jit(solution)/shard_map/ppermute | solution.py:241
  15.9 0.7 collective-permute-start.4
  16.6 1.7 %collective-permute-start.1 = (f32[4,128,128]{2,1,0:T(8,128)S(1)}, f32[4,128,128]{2,1,0:T(8,128)S(1)}, u32[]{:S(2)}, u32[]{:S(2)}) collective-permute-start(f32[4,128,128]{2,1,0:T(8,128)S(1)} %get-tuple-element.26.rest_0_), channel_id=1, source_target_pairs={{0,4},{2,6},{8,12},{10,14},{16,20},{18,22},{24,28},{26,30},{4,0},{... | collective-permute-start | bytes 786440 | tf_op jit(solution)/shard_map/ppermute | solution.py:241
  18.3 0.0 copy-done.4
  18.3 2.7 %local.2.rest_4_ = f32[3,256,1024]{2,1,0:T(8,128)S(1)} custom-call(s32[8]{0:T(128)S(1)} %copy-done.6, bf16[256,2048]{1,0:T(8,128)(2,1)S(1)} %copy-done.4, bf16[256,2048]{1,0:T(8,128)(2,1)S(1)} %copy-done, bf16[256,2048]{1,0:T(8,128)(2,1)S(1)} %copy-done.1, bf16[256,2048]{1,0:T(8,128)(2,1)S(1)} %copy-done.2, f32[4,128,128]{2,1,0:T(8,128)S(1)} %get-tuple-element.26.rest_0_), custom_call_target="tpu_custom_call" | custom-call | bytes 1024 | tf_op jit(solution)/shard_map/local/pallas_call | solution.py:221
  21.0 0.0 collective-permute-done.2.rest_1_
  21.0 6.7 %collective-permute-done.3.rest_2_ = f32[4,128,128]{2,1,0:T(8,128)S(1)} collective-permute-done((f32[4,128,128]{2,1,0:T(8,128)S(1)}, f32[4,128,128]{2,1,0:T(8,128)S(1)}, u32[]{:S(2)}, u32[]{:S(2)}) %collective-permute-start.3) | collective-permute-done | bytes 262176 | tf_op jit(solution)/shard_map/ppermute | solution.py:241
  27.7 0.0 collective-permute-done.4.rest_3_
  27.7 0.0 collective-permute-done.1.rest_0_
  27.7 0.8 join.2
  28.5 0.1 collective-permute-start.5
  28.6 0.0 collective-permute-done.7.got
  28.6 0.7 pair.3
  29.3 1.5 %collective-permute-start.8 = (f32[4,128,128]{2,1,0:T(8,128)S(1)}, f32[4,128,128]{2,1,0:T(8,128)S(1)}, u32[]{:S(2)}, u32[]{:S(2)}) collective-permute-start(f32[4,128,128]{2,1,0:T(8,128)S(1)} %get-tuple-element.35), channel_id=1, source_target_pairs={{0,4},{2,6},{8,12},{10,14},{16,20},{18,22},{24,28},{26,30},{4,0},{... | collective-permute-start | bytes 786440 | tf_op jit(solution)/shard_map/ppermute | solution.py:241
  30.8 0.7 collective-permute-start.9
  31.5 3.4 %collective-permute-start.10 = (f32[4,128,128]{2,1,0:T(8,128)S(1)}, f32[4,128,128]{2,1,0:T(8,128)S(1)}, u32[]{:S(2)}, u32[]{:S(2)}) collective-permute-start(f32[4,128,128]{2,1,0:T(8,128)S(1)} %get-tuple-element.37), channel_id=1, source_target_pairs={{0,8},{2,10},{4,12},{6,14},{16,24},{18,26},{20,28},{22,30},{8,0},{... | collective-permute-start | bytes 786440 | tf_op jit(solution)/shard_map/ppermute | solution.py:241
  34.8 0.7 collective-permute-start.11
  35.5 0.0 collective-permute-done.5.got
  35.5 2.0 %carry.2 = (bf16[3,128,1024]{2,1,0:T(8,128)(2,1)S(1)}, bf16[3,128,1024]{2,1,0:T(8,128)(2,1)S(1)}) custom-call(s32[8]{0:T(128)S(1)} %copy-done.6, bf16[256,2048]{1,0:T(8,128)(2,1)S(1)} %copy-done, bf16[256,2048]{1,0:T(8,128)(2,1)S(1)} %copy-done.1, bf16[256,2048]{1,0:T(8,128)(2,1)S(1)} %copy-done.2, f32[3,256,1024]{2,1,0:T(8,128)S(1)} %local.2.rest_4_, ...), custom_call_target="tpu_custom_call" | custom-call | bytes 1024 | tf_op jit(solution)/shard_map/carry/pallas_call | solution.py:221
  37.6 2.7 %local.3.rest_4_ = f32[3,256,1024]{2,1,0:T(8,128)S(1)} custom-call(s32[8]{0:T(128)S(1)} %copy-done.6, bf16[256,2048]{1,0:T(8,128)(2,1)S(1)} %copy-done.4, bf16[256,2048]{1,0:T(8,128)(2,1)S(1)} %copy-done, bf16[256,2048]{1,0:T(8,128)(2,1)S(1)} %copy-done.1, bf16[256,2048]{1,0:T(8,128)(2,1)S(1)} %copy-done.2, ...), custom_call_target="tpu_custom_call" | custom-call | bytes 1024 | tf_op jit(solution)/shard_map/local/pallas_call | solution.py:221
  40.3 2.4 %collective-permute-done.8.rest_0_ = f32[4,128,128]{2,1,0:T(8,128)S(1)} collective-permute-done((f32[4,128,128]{2,1,0:T(8,128)S(1)}, f32[4,128,128]{2,1,0:T(8,128)S(1)}, u32[]{:S(2)}, u32[]{:S(2)}) %collective-permute-start.8) | collective-permute-done | bytes 262176 | tf_op jit(solution)/shard_map/ppermute | solution.py:241
  42.6 0.0 collective-permute-done.9.rest_1_
  42.6 4.2 %collective-permute-done.10.rest_2_ = f32[4,128,128]{2,1,0:T(8,128)S(1)} collective-permute-done((f32[4,128,128]{2,1,0:T(8,128)S(1)}, f32[4,128,128]{2,1,0:T(8,128)S(1)}, u32[]{:S(2)}, u32[]{:S(2)}) %collective-permute-start.10) | collective-permute-done | bytes 262176 | tf_op jit(solution)/shard_map/ppermute | solution.py:241
  46.8 0.0 collective-permute-done.11.rest_3_
  46.8 0.8 join.3
  47.6 0.1 collective-permute-start.12
  47.7 1.6 %collective-permute-start.6 = (bf16[3,128,1024]{2,1,0:T(8,128)(2,1)S(1)}, bf16[3,128,1024]{2,1,0:T(8,128)(2,1)S(1)}, u32[]{:S(2)}, u32[]{:S(2)}) collective-permute-start(bf16[3,128,1024]{2,1,0:T(8,128)(2,1)S(1)} %get-tuple-element.33), channel_id=1, source_target_pairs={{0,1},{1,0},{2,3},{3,2},{4,5},{5,4},{6,7},{7,6},{8,9},{9,8},{10,11... | collective-permute-start | bytes 2359304 | tf_op jit(solution)/shard_map/ppermute | solution.py:247
  49.3 0.3 collective-permute-done.12.got
  49.6 2.0 %carry.3 = (bf16[3,128,1024]{2,1,0:T(8,128)(2,1)S(1)}, bf16[3,128,1024]{2,1,0:T(8,128)(2,1)S(1)}) custom-call(s32[8]{0:T(128)S(1)} %copy-done.6, bf16[256,2048]{1,0:T(8,128)(2,1)S(1)} %copy-done, bf16[256,2048]{1,0:T(8,128)(2,1)S(1)} %copy-done.1, bf16[256,2048]{1,0:T(8,128)(2,1)S(1)} %copy-done.2, f32[3,256,1024]{2,1,0:T(8,128)S(1)} %local.3.rest_4_, ...), custom_call_target="tpu_custom_call" | custom-call | bytes 1024 | tf_op jit(solution)/shard_map/carry/pallas_call | solution.py:221
  51.7 1.6 %collective-permute-start.13 = (bf16[3,128,1024]{2,1,0:T(8,128)(2,1)S(1)}, bf16[3,128,1024]{2,1,0:T(8,128)(2,1)S(1)}, u32[]{:S(2)}, u32[]{:S(2)}) collective-permute-start(bf16[3,128,1024]{2,1,0:T(8,128)(2,1)S(1)} %get-tuple-element.42), channel_id=1, source_target_pairs={{0,1},{1,0},{2,3},{3,2},{4,5},{5,4},{6,7},{7,6},{8,9},{9,8},{10,11... | collective-permute-start | bytes 2359304 | tf_op jit(solution)/shard_map/ppermute | solution.py:247
  53.2 14.9 %collective-permute-done.6.refs_1_ = bf16[3,128,1024]{2,1,0:T(8,128)(2,1)S(1)} collective-permute-done((bf16[3,128,1024]{2,1,0:T(8,128)(2,1)S(1)}, bf16[3,128,1024]{2,1,0:T(8,128)(2,1)S(1)}, u32[]{:S(2)}, u32[]{:S(2)}) %collective-permute-start.6) | collective-permute-done | bytes 786464 | tf_op jit(solution)/shard_map/ppermute | solution.py:247
  68.1 16.4 %collective-permute-done.13.refs_3_ = bf16[3,128,1024]{2,1,0:T(8,128)(2,1)S(1)} collective-permute-done((bf16[3,128,1024]{2,1,0:T(8,128)(2,1)S(1)}, bf16[3,128,1024]{2,1,0:T(8,128)(2,1)S(1)}, u32[]{:S(2)}, u32[]{:S(2)}) %collective-permute-start.13) | collective-permute-done | bytes 786464 | tf_op jit(solution)/shard_map/ppermute | solution.py:247
  84.5 1.8 %place.1 = (bf16[128,4096]{1,0:T(8,128)(2,1)}, bf16[128,4096]{1,0:T(8,128)(2,1)}, bf16[128,4096]{1,0:T(8,128)(2,1)}) custom-call(bf16[3,128,1024]{2,1,0:T(8,128)(2,1)S(1)} %get-tuple-element.32.rest_0_.refs_0_, bf16[3,128,1024]{2,1,0:T(8,128)(2,1)S(1)} %collective-permute-done.6.refs_1_, bf16[3,128,1024]{2,1,0:T(8,128)(2,1)S(1)} %get-tuple-element.41.refs_2_, ...), custom_call_target="tpu_custom_call" | custom-call | bytes 6291456 | tf_op jit(solution)/shard_map/place/pallas_call | solution.py:316
Async XLA Ops:
  0.6 4.4 %copy-start.6 = (s32[8]{0:T(128)S(1)}, s32[8]{0:T(128)}, u32[]{:S(2)}) copy-start(s32[8]{0:T(128)} %lengths.19) | copy-start | bytes 100
  0.6 4.4 %copy-start.2 = (bf16[256,2048]{1,0:T(8,128)(2,1)S(1)}, bf16[256,2048]{1,0:T(8,128)(2,1)}, u32[]{:S(2)}) copy-start(bf16[256,2048]{1,0:T(8,128)(2,1)} %g.11) | copy-start | bytes 3145732
  0.7 4.4 %copy-start.1 = (bf16[256,2048]{1,0:T(8,128)(2,1)S(1)}, bf16[256,2048]{1,0:T(8,128)(2,1)}, u32[]{:S(2)}) copy-start(bf16[256,2048]{1,0:T(8,128)(2,1)} %v.11) | copy-start | bytes 3145732
  0.7 4.4 %copy-start = (bf16[256,2048]{1,0:T(8,128)(2,1)S(1)}, bf16[256,2048]{1,0:T(8,128)(2,1)}, u32[]{:S(2)}) copy-start(bf16[256,2048]{1,0:T(8,128)(2,1)} %k.11) | copy-start | bytes 3145732
  4.6 4.2 %collective-permute-start = (f32[2,4,128,128]{3,2,1,0:T(8,128)}, f32[2,4,128,128]{3,2,1,0:T(8,128)S(1)}, u32[]{:S(2)}, u32[]{:S(2)}) collective-permute-start(f32[2,4,128,128]{3,2,1,0:T(8,128)} %get-tuple-element.24), channel_id=1, source_target_pairs={{0,2},{2,0},{4,6},{6,4},{8,10},{10,8},{12,14},{14,12},{16,18},{18,... | collective-permute-start | bytes 1572872 | tf_op jit(solution)/shard_map/ppermute | solution.py:233
  5.1 1.2 %copy-start.3 = (bf16[256,2048]{1,0:T(8,128)(2,1)S(1)}, bf16[256,2048]{1,0:T(8,128)(2,1)}, u32[]{:S(2)}) copy-start(bf16[256,2048]{1,0:T(8,128)(2,1)} %q.7) | copy-start | bytes 3145732
  6.3 1.0 %copy-start.5 = (f32[2,4,128,128]{3,2,1,0:T(8,128)S(1)}, f32[2,4,128,128]{3,2,1,0:T(8,128)}, u32[]{:S(2)}) copy-start(f32[2,4,128,128]{3,2,1,0:T(8,128)} %get-tuple-element.23.rest_0_.kept) | copy-start | bytes 1572868
  7.4 11.0 %copy-start.4 = (bf16[256,2048]{1,0:T(8,128)(2,1)S(1)}, bf16[256,2048]{1,0:T(8,128)(2,1)}, u32[]{:S(2)}) copy-start(bf16[256,2048]{1,0:T(8,128)(2,1)} %q.7) | copy-start | bytes 3145732
  8.7 19.9 %collective-permute-start.7 = (f32[2,4,128,128]{3,2,1,0:T(8,128)S(1)}, f32[2,4,128,128]{3,2,1,0:T(8,128)S(1)}, u32[]{:S(2)}, u32[]{:S(2)}) collective-permute-start(f32[2,4,128,128]{3,2,1,0:T(8,128)S(1)} %get-tuple-element.34), channel_id=1, source_target_pairs={{0,2},{2,0},{4,6},{6,4},{8,10},{10,8},{12,14},{14,12},{16,18},{18,... | collective-permute-start | bytes 1572872 | tf_op jit(solution)/shard_map/ppermute | solution.py:233
  9.5 11.5 %collective-permute-start.2 = (f32[4,128,128]{2,1,0:T(8,128)S(1)}, f32[4,128,128]{2,1,0:T(8,128)S(1)}, u32[]{:S(2)}, u32[]{:S(2)}) collective-permute-start(f32[4,128,128]{2,1,0:T(8,128)S(1)} %get-tuple-element.27), channel_id=1, source_target_pairs={{4,8},{6,10},{12,16},{14,18},{20,24},{22,26},{8,4},{10,6},{16,12},... | collective-permute-start | bytes 786440 | tf_op jit(solution)/shard_map/ppermute | solution.py:241
  10.2 17.5 %collective-permute-start.3 = (f32[4,128,128]{2,1,0:T(8,128)S(1)}, f32[4,128,128]{2,1,0:T(8,128)S(1)}, u32[]{:S(2)}, u32[]{:S(2)}) collective-permute-start(f32[4,128,128]{2,1,0:T(8,128)S(1)} %get-tuple-element.28), channel_id=1, source_target_pairs={{0,8},{2,10},{4,12},{6,14},{16,24},{18,26},{20,28},{22,30},{8,0},{... | collective-permute-start | bytes 786440 | tf_op jit(solution)/shard_map/ppermute | solution.py:241
  15.9 11.8 %collective-permute-start.4 = (f32[4,128,128]{2,1,0:T(8,128)S(1)}, f32[4,128,128]{2,1,0:T(8,128)S(1)}, u32[]{:S(2)}, u32[]{:S(2)}) collective-permute-start(f32[4,128,128]{2,1,0:T(8,128)S(1)} %get-tuple-element.29), channel_id=1, source_target_pairs={{8,16},{10,18},{12,20},{14,22},{16,8},{18,10},{20,12},{22,14},{9,1... | collective-permute-start | bytes 786440 | tf_op jit(solution)/shard_map/ppermute | solution.py:241
  16.6 11.1 %collective-permute-start.1 = (f32[4,128,128]{2,1,0:T(8,128)S(1)}, f32[4,128,128]{2,1,0:T(8,128)S(1)}, u32[]{:S(2)}, u32[]{:S(2)}) collective-permute-start(f32[4,128,128]{2,1,0:T(8,128)S(1)} %get-tuple-element.26.rest_0_), channel_id=1, source_target_pairs={{0,4},{2,6},{8,12},{10,14},{16,20},{18,22},{24,28},{26,30},{4,0},{... | collective-permute-start | bytes 786440 | tf_op jit(solution)/shard_map/ppermute | solution.py:241
  28.5 7.0 %collective-permute-start.5 = (f32[2,4,128,128]{3,2,1,0:T(8,128)S(1)}, f32[2,4,128,128]{3,2,1,0:T(8,128)S(1)}, u32[]{:S(2)}, u32[]{:S(2)}) collective-permute-start(f32[2,4,128,128]{3,2,1,0:T(8,128)S(1)} %get-tuple-element.31), channel_id=1, source_target_pairs={{0,2},{2,0},{4,6},{6,4},{8,10},{10,8},{12,14},{14,12},{16,18},{18,... | collective-permute-start | bytes 1572872 | tf_op jit(solution)/shard_map/ppermute | solution.py:233
  29.3 13.3 %collective-permute-start.8 = (f32[4,128,128]{2,1,0:T(8,128)S(1)}, f32[4,128,128]{2,1,0:T(8,128)S(1)}, u32[]{:S(2)}, u32[]{:S(2)}) collective-permute-start(f32[4,128,128]{2,1,0:T(8,128)S(1)} %get-tuple-element.35), channel_id=1, source_target_pairs={{0,4},{2,6},{8,12},{10,14},{16,20},{18,22},{24,28},{26,30},{4,0},{... | collective-permute-start | bytes 786440 | tf_op jit(solution)/shard_map/ppermute | solution.py:241
  30.8 11.8 %collective-permute-start.9 = (f32[4,128,128]{2,1,0:T(8,128)S(1)}, f32[4,128,128]{2,1,0:T(8,128)S(1)}, u32[]{:S(2)}, u32[]{:S(2)}) collective-permute-start(f32[4,128,128]{2,1,0:T(8,128)S(1)} %get-tuple-element.36), channel_id=1, source_target_pairs={{4,8},{6,10},{12,16},{14,18},{20,24},{22,26},{8,4},{10,6},{16,12},... | collective-permute-start | bytes 786440 | tf_op jit(solution)/shard_map/ppermute | solution.py:241
  31.5 15.3 %collective-permute-start.10 = (f32[4,128,128]{2,1,0:T(8,128)S(1)}, f32[4,128,128]{2,1,0:T(8,128)S(1)}, u32[]{:S(2)}, u32[]{:S(2)}) collective-permute-start(f32[4,128,128]{2,1,0:T(8,128)S(1)} %get-tuple-element.37), channel_id=1, source_target_pairs={{0,8},{2,10},{4,12},{6,14},{16,24},{18,26},{20,28},{22,30},{8,0},{... | collective-permute-start | bytes 786440 | tf_op jit(solution)/shard_map/ppermute | solution.py:241
  34.8 12.0 %collective-permute-start.11 = (f32[4,128,128]{2,1,0:T(8,128)S(1)}, f32[4,128,128]{2,1,0:T(8,128)S(1)}, u32[]{:S(2)}, u32[]{:S(2)}) collective-permute-start(f32[4,128,128]{2,1,0:T(8,128)S(1)} %get-tuple-element.38), channel_id=1, source_target_pairs={{8,16},{10,18},{12,20},{14,22},{16,8},{18,10},{20,12},{22,14},{9,1... | collective-permute-start | bytes 786440 | tf_op jit(solution)/shard_map/ppermute | solution.py:241
  47.6 2.0 %collective-permute-start.12 = (f32[2,4,128,128]{3,2,1,0:T(8,128)S(1)}, f32[2,4,128,128]{3,2,1,0:T(8,128)S(1)}, u32[]{:S(2)}, u32[]{:S(2)}) collective-permute-start(f32[2,4,128,128]{3,2,1,0:T(8,128)S(1)} %get-tuple-element.40), channel_id=1, source_target_pairs={{0,2},{2,0},{4,6},{6,4},{8,10},{10,8},{12,14},{14,12},{16,18},{18,... | collective-permute-start | bytes 1572872 | tf_op jit(solution)/shard_map/ppermute | solution.py:233
  47.7 20.4 %collective-permute-start.6 = (bf16[3,128,1024]{2,1,0:T(8,128)(2,1)S(1)}, bf16[3,128,1024]{2,1,0:T(8,128)(2,1)S(1)}, u32[]{:S(2)}, u32[]{:S(2)}) collective-permute-start(bf16[3,128,1024]{2,1,0:T(8,128)(2,1)S(1)} %get-tuple-element.33), channel_id=1, source_target_pairs={{0,1},{1,0},{2,3},{3,2},{4,5},{5,4},{6,7},{7,6},{8,9},{9,8},{10,11... | collective-permute-start | bytes 2359304 | tf_op jit(solution)/shard_map/ppermute | solution.py:247
  51.7 32.9 %collective-permute-start.13 = (bf16[3,128,1024]{2,1,0:T(8,128)(2,1)S(1)}, bf16[3,128,1024]{2,1,0:T(8,128)(2,1)S(1)}, u32[]{:S(2)}, u32[]{:S(2)}) collective-permute-start(bf16[3,128,1024]{2,1,0:T(8,128)(2,1)S(1)} %get-tuple-element.42), channel_id=1, source_target_pairs={{0,1},{1,0},{2,3},{3,2},{4,5},{5,4},{6,7},{7,6},{8,9},{9,8},{10,11... | collective-permute-start | bytes 2359304 | tf_op jit(solution)/shard_map/ppermute | solution.py:247

commit v3 on v2

v3 whole, which is shorter than its diff:
```python
import functools

import jax
import jax.numpy as jnp
from jax import lax
from jax.experimental import pallas as pl
from jax.experimental.pallas import tpu as pltpu
from jax.sharding import PartitionSpec as P

HEAD_DIM = 128
MOST = 1024
GROUP = 4
CUTS = (4, 4, 4, 4)
LINK = jnp.bfloat16
VMEM_LIMIT = 16 * 1024 * 1024
GRAD_LIMIT = 48 * 1024 * 1024
FIRST_LIMIT = 52 * 1024 * 1024
NT = (((1,), (1,)), ((), ()))
TN = (((0,), (0,)), ((), ()))
NN = (((1,), (0,)), ((), ()))


def dot(a, b, dims):
    return lax.dot_general(a, b, dims, preferred_element_type=jnp.float32)


def doc_at(meta, ndocs, position):
    start, begin, end = jnp.int32(0), jnp.int32(0), jnp.int32(0)
    for i in range(ndocs):
        stop = start + meta[i]
        begin = jnp.where(start <= position, start, begin)
        end = jnp.where(start <= position, stop, end)
        start = stop
    return begin, end


def block_range(meta, ndocs, base, rows):
    begin0, end0 = doc_at(meta, ndocs, base)
    begin1, end1 = doc_at(meta, ndocs, base + rows - 1)
    first = jnp.where(begin0 < base, end0, base) - base
    return begin0, end0, begin1, end1, first, begin1 - base


def goes_up(place, hop):
    return lax.rem(lax.div(lax.div(place, 2), hop), 2) == 0


def state_kernel(lengths, q, k, v, g, kept, sent, *, ndocs, rows, heads):
    place = lax.axis_index("seq")
    first_core = lax.rem(place, 2) == 0
    _, _, _, _, first, last = block_range(lengths, ndocs, place * rows, rows)
    order = lax.broadcasted_iota(jnp.int32, (rows, HEAD_DIM), 0)
    first_rows, last_rows = order < first, order >= last
    zero = jnp.zeros((), q.dtype)

    def one(h):
        cols = slice(h * HEAD_DIM, (h + 1) * HEAD_DIM)
        tail = dot(jnp.where(last_rows, k[:, cols], zero), v[:, cols], TN)
        return tail, dot(jnp.where(first_rows, q[:, cols], zero), g[:, cols], TN)

    for i in range(heads // 2):
        for which, (low, high) in enumerate(zip(one(2 * i), one(2 * i + 1))):
            kept[which, i] = jnp.where(first_core, low, high)
            sent[which, i] = jnp.where(first_core, high, low)


def pair_parts(kept, got, first_core, i):
    tail_even = jnp.where(first_core, kept[0, i], got[0, i])
    tail_odd = jnp.where(first_core, got[0, i], kept[0, i])
    head_even = jnp.where(first_core, kept[1, i], got[1, i])
    head_odd = jnp.where(first_core, got[1, i], kept[1, i])
    return tail_even, tail_odd, head_even, head_odd


def pair_kernel(lengths, kept, got, *sent, ndocs, rows, count, hops):
    place = lax.axis_index("seq")
    first_core = lax.rem(place, 2) == 0
    even = (place - lax.rem(place, 2)) * rows
    odd = even + rows
    _, even_e0 = doc_at(lengths, ndocs, even)
    odd_b1, _ = doc_at(lengths, ndocs, odd + rows - 1)
    tail_joins = jnp.where(odd_b1 < odd, 1.0, 0.0)
    head_joins = jnp.where(even_e0 > odd, 1.0, 0.0)
    ups = [goes_up(place, hop) for hop in range(1, hops + 1)]
    for i in range(count):
        tail_even, tail_odd, head_even, head_odd = pair_parts(kept, got, first_core, i)
        tail = tail_odd + tail_joins * tail_even
        head = head_even + head_joins * head_odd
        for hop in range(hops):
            sent[2 * hop][i] = jnp.where(ups[hop], tail, head).astype(LINK)
            sent[2 * hop + 1][i] = jnp.where(ups[hop], head, tail).astype(LINK)


def join_kernel(lengths, kept, got, *rest, ndocs, rows, counts, hops):
    came, mine, theirs = rest[:2 * hops], rest[-2 * len(counts):-len(counts)], rest[-len(counts):]
    place = lax.axis_index("seq")
    first_core = lax.rem(place, 2) == 0
    even = (place - lax.rem(place, 2)) * rows
    odd = even + rows
    even_b0, _ = doc_at(lengths, ndocs, even)
    _, even_e1 = doc_at(lengths, ndocs, odd - 1)
    odd_b0, _ = doc_at(lengths, ndocs, odd)
    _, odd_e1 = doc_at(lengths, ndocs, odd + rows - 1)

    def one(flag):
        return jnp.where(flag, 1.0, 0.0)

    ups = [goes_up(place, hop) for hop in range(1, hops + 1)]
    tail_w = [one(even - hop * 2 * rows > even_b0) for hop in range(hops)]
    head_w = [one(odd + rows + hop * 2 * rows < odd_e1) for hop in range(hops)]
    state_from_tail, state_from_pair = one(odd > odd_b0), one(even > odd_b0)
    grad_from_head, grad_from_pair = one(odd < even_e1), one(odd + rows < even_e1)
    for c, count in enumerate(counts):
        for n in range(count):
            i = sum(counts[:c]) + n
            tail_even, _, _, head_odd = pair_parts(kept, got, first_core, i)
            state_even, grad_odd = 0.0, 0.0
            for hop in range(hops):
                a, b = (came[2 * hop + turn][i].astype(jnp.float32) for turn in range(2))
                state_even = state_even + tail_w[hop] * jnp.where(ups[hop], b, a)
                grad_odd = grad_odd + head_w[hop] * jnp.where(ups[hop], a, b)
            state_odd = state_from_tail * tail_even + state_from_pair * state_even
            grad_even = grad_from_head * head_odd + grad_from_pair * grad_odd
            mine[c][0, n] = jnp.where(first_core, state_even, state_odd)
            mine[c][1, n] = jnp.where(first_core, grad_even, grad_odd)
            theirs[c][0, n] = jnp.where(first_core, state_odd, state_even)
            theirs[c][1, n] = jnp.where(first_core, grad_odd, grad_even)


def split(a, axis):
    high = a.astype(jnp.bfloat16)
    return jnp.concatenate([high, (a - high.astype(jnp.float32)).astype(jnp.bfloat16)], axis=axis)


def grad_kernel(lengths, q, k, v, g, mine, got, *rest, ndocs, rows, heads, groups):
    outs, lower, upper, done = rest[-3 - groups:-3], rest[-3], rest[-2], rest[-1]
    place, column = lax.axis_index("seq"), lax.axis_index("head")
    base = place * rows

    @pl.when(pl.program_id(0) == 0)
    def _():
        line = lax.broadcasted_iota(jnp.int32, (rows, rows), 0)
        across = lax.broadcasted_iota(jnp.int32, (rows, rows), 1)
        begin_line = jnp.zeros((rows, rows), jnp.int32)
        begin_across = jnp.zeros((rows, rows), jnp.int32)
        start = jnp.int32(0) - base
        for i in range(ndocs):
            begin_line = jnp.where(line >= start, start, begin_line)
            begin_across = jnp.where(across >= start, start, begin_across)
            start = start + lengths[i]
        lower[...] = jnp.where((across <= line) & (across >= begin_line), 1, 0)
        upper[...] = jnp.where((line <= across) & (line >= begin_across), 1, 0)

    first_core = lax.rem(place, 2) == 0
    _, _, _, _, first, last = block_range(lengths, ndocs, base, rows)
    order = lax.broadcasted_iota(jnp.int32, (rows, HEAD_DIM), 0)
    first_rows, last_rows = order < first, order >= last
    in_lower, in_upper = lower[...] == 1, upper[...] == 1
    for h in range(heads):
        cols = slice(h * HEAD_DIM, (h + 1) * HEAD_DIM)
        here = first_core if h % 2 == 0 else jnp.logical_not(first_core)
        state, grad = (jnp.where(here, mine[which, h // 2], got[which, h // 2]) for which in range(2))
        qh, kh, vh, gh = (ref[:, cols] for ref in (q, k, v, g))
        k2, v2, g2 = (jnp.concatenate([a, a], axis=1) for a in (kh, vh, gh))
        weight_gv = jnp.where(in_lower, dot(gh, vh, NT), 0.0).astype(jnp.bfloat16)
        weight_vg = jnp.where(in_upper, dot(vh, gh, NT), 0.0).astype(jnp.bfloat16)
        weight_kq = jnp.where(in_upper, dot(kh, qh, NT), 0.0).astype(jnp.bfloat16)
        carry_q = jnp.where(first_rows, dot(g2, split(state, 1), NT), 0.0)
        carry_k = jnp.where(last_rows, dot(v2, split(grad, 1), NT), 0.0)
        carry_v = jnp.where(last_rows, dot(k2, split(grad, 0), NN), 0.0)
        done[0, :, cols] = (dot(weight_gv, kh, NN) + carry_q).astype(jnp.bfloat16)
        done[1, :, cols] = (dot(weight_vg, qh, NN) + carry_k).astype(jnp.bfloat16)
        done[2, :, cols] = (dot(weight_kq, gh, NN) + carry_v).astype(jnp.bfloat16)
    part = rows // groups
    for j in range(groups):
        at = pl.ds(pl.multiple_of(lax.rem(column + j, groups) * part, part), part)
        for i in range(3):
            outs[j][i] = done[i, at, :]


def place_kernel(*refs, groups, offset, cw, width):
    parts, outs, sems = refs[:groups], refs[-4:-1], refs[-1]
    column = lax.axis_index("head")
    copies = []
    for j in range(groups):
        start = pl.multiple_of(lax.rem(column + groups - j, groups) * width + offset, 128)
        for i in range(3):
            copies.append(pltpu.make_async_copy(parts[j].at[i], outs[i].at[:, pl.ds(start, cw)], sems.at[len(copies)]))
            copies[-1].start()
    for copy in copies:
        copy.wait()


def cuts_of(width):
    heads = width // HEAD_DIM
    sizes = CUTS if sum(CUTS) == heads else (2,) * (heads // 2)
    offsets = [sum(sizes[:c]) for c in range(len(sizes))]
    return [(o * HEAD_DIM, s * HEAD_DIM) for o, s in zip(offsets, sizes)]


def shards(queries, keys, values, out_grad, doc_lengths):
    rows, width = queries.shape
    ndocs = doc_lengths.shape[0]
    seq, groups = lax.axis_size("seq"), lax.axis_size("head")
    pairs = seq // 2
    hops = -(-MOST // (2 * rows))
    cuts = cuts_of(width)
    group = GROUP if width % (GROUP * HEAD_DIM) == 0 else 2
    gw, step = group * HEAD_DIM, 2 * HEAD_DIM
    count = width // HEAD_DIM // 2
    counts = [cw // HEAD_DIM // 2 for _, cw in cuts]
    part = rows // groups
    anywhere = pl.BlockSpec(memory_space=pl.ANY)
    in_vmem = pl.BlockSpec(memory_space=pltpu.VMEM)
    in_smem = pl.BlockSpec(memory_space=pltpu.SMEM)
    f32, bf16 = jnp.float32, jnp.bfloat16
    inputs = (queries, keys, values, out_grad)
    sizes = dict(ndocs=ndocs, rows=rows)
    cheap = pl.CostEstimate(flops=0, bytes_accessed=1024, transcendentals=0)

    def shape_of(*dims, dtype=f32):
        return jax.ShapeDtypeStruct(dims, dtype)

    def call(name, kernel, args, outs, scratch=(), after=()):
        return pl.pallas_call(
            kernel, in_specs=[in_smem] + [in_vmem] * len(args) + [anywhere] * len(after), out_specs=[in_vmem] * len(outs), out_shape=outs,
            scratch_shapes=list(scratch), cost_estimate=cheap,
            compiler_params=pltpu.CompilerParams(vmem_limit_bytes=VMEM_LIMIT), name=name,
        )(doc_lengths, *args, *after)

    def swap_cores(a):
        return lax.ppermute(a, "seq", [(b, b ^ 1) for b in range(seq)])

    def swap_pairs(sent):
        came = []
        for hop in range(1, hops + 1):
            for turn in range(2):
                lower = [m for m in range(pairs - hop) if (m // hop) % 2 == turn]
                perm = [(2 * m + core, 2 * (m + hop) + core) for m in lower for core in range(2)]
                came.append(lax.ppermute(sent[2 * (hop - 1) + turn], "seq", perm + [(b, a) for a, b in perm]))
        return came

    def send_rows(outs):
        arrived = list(outs[:1])
        for j in range(1, groups):
            arrived.append(lax.ppermute(outs[j], "head", [(x, (x + j) % groups) for x in range(groups)]))
        return arrived

    square = (HEAD_DIM, HEAD_DIM)
    state_block = pl.BlockSpec((2, group // 2) + square, lambda c, lengths: (0, c, 0, 0))
    kept, sent = pl.pallas_call(
        functools.partial(state_kernel, heads=group, **sizes),
        grid_spec=pltpu.PrefetchScalarGridSpec(
            num_scalar_prefetch=1, grid=(width // gw,),
            in_specs=[pl.BlockSpec((rows, gw), lambda c, lengths: (0, c))] * 4, out_specs=[state_block] * 2,
        ),
        out_shape=[shape_of(2, count, *square)] * 2, cost_estimate=cheap,
        compiler_params=pltpu.CompilerParams(vmem_limit_bytes=FIRST_LIMIT), name="states",
    )(doc_lengths, *inputs)
    got = swap_cores(sent)
    sent = call(
        "pair", functools.partial(pair_kernel, count=count, hops=hops, **sizes), (kept, got),
        [shape_of(count, *square, dtype=LINK)] * (2 * hops),
    )
    came = swap_pairs(sent)
    joined = call(
        "join", functools.partial(join_kernel, counts=counts, hops=hops, **sizes), (kept, got, *came),
        [shape_of(2, n, *square) for n in counts] * 2,
    )
    parts, last = [], joined[0]
    for c, (offset, cw) in enumerate(cuts):
        mine, theirs = joined[c], joined[len(cuts) + c]
        block = pl.BlockSpec((rows, step), lambda s, lengths, at=offset // step: (0, at + s))
        pair_block = pl.BlockSpec((2, 1) + square, lambda s, lengths: (0, s, 0, 0))
        out_block = pl.BlockSpec((3, part, step), lambda s, lengths: (0, 0, s))
        outs = pl.pallas_call(
            functools.partial(grad_kernel, heads=2, groups=groups, **sizes),
            grid_spec=pltpu.PrefetchScalarGridSpec(
                num_scalar_prefetch=1, grid=(cw // step,), in_specs=[block] * 4 + [pair_block] * 2 + [anywhere],
                out_specs=[out_block] * groups,
                scratch_shapes=[pltpu.VMEM((rows, rows), jnp.int32)] * 2 + [pltpu.VMEM((3, rows, step), bf16)],
            ),
            out_shape=[shape_of(3, part, cw, dtype=bf16)] * groups, cost_estimate=cheap,
            compiler_params=pltpu.CompilerParams(vmem_limit_bytes=GRAD_LIMIT), name="grads",
        )(doc_lengths, *inputs, mine, swap_cores(theirs), last)
        last = outs[0]
        parts += send_rows(outs)

    placed = []
    for c, (offset, cw) in enumerate(cuts):
        some = parts[c * groups:(c + 1) * groups]
        placed = pl.pallas_call(
            functools.partial(place_kernel, groups=groups, offset=offset, cw=cw, width=width),
            grid_spec=pl.GridSpec(
                grid=(1,), in_specs=[anywhere] * (groups + len(placed)), out_specs=[anywhere] * 3,
                scratch_shapes=[pltpu.SemaphoreType.DMA((3 * groups,))],
            ),
            out_shape=[shape_of(part, width * groups, dtype=bf16)] * 3,
            input_output_aliases={groups + i: i for i in range(len(placed))},
            cost_estimate=cheap,
            compiler_params=pltpu.CompilerParams(vmem_limit_bytes=VMEM_LIMIT), name="place",
        )(*some, *placed)
    return tuple(placed)


def solution(mesh):
    return jax.shard_map(
        shards,
        mesh=mesh,
        in_specs=(P("seq", "head"), P("seq", "head"), P("seq", "head"), P("seq", "head"), P()),
        out_specs=(P(("seq", "head"), None), P(("seq", "head"), None), P(("seq", "head"), None)),
        check_vma=False,
    )
```

time: 86.5 us -> 71.8 us (0.83)
  waiting for transfers between devices: 44.9 us -> 35 us
  starting transfers between devices: 18.8 us -> 13.1 us
  Pallas kernels: 19.5 us -> 22.1 us
  local copies, waits for them, and re-layouts: 2.28 us -> 0.67 us
    ppermute x2 -> x4, waiting for transfers between devices: 31.3 us -> 20.9 us  [send_rows(): lax.ppermute(outs[j], 'head', [(x, (x + j) % groups) for x in range(group...]
    ppermute x8 -> x4, starting transfers between devices: 14.9 us -> 7.3 us  [swap_pairs(): lax.ppermute(sent[2 * (hop - 1) + turn], 'seq', perm + [(b, a) for a, b i...]
    ppermute x4 -> x5, waiting for transfers between devices: 0.35 us -> 3.02 us  [swap_cores(): return lax.ppermute(a, 'seq', [(b, b ^ 1) for b in range(seq)])]
    pallas_call x11, Pallas kernels: 19.5 us -> 22.1 us  [the longest x4 11.3 us: shards(): pl.pallas_call(functools.partial(grad_kernel, heads=2, groups=groups, **s...]
    ppermute x8 -> x4, waiting for transfers between devices: 13.2 us -> 11.1 us  [swap_pairs(): lax.ppermute(sent[2 * (hop - 1) + turn], 'seq', perm + [(b, a) for a, b i...]
    unnamed x14 -> x12, local copies, waits for them, and re-layouts: 2.28 us -> 0.67 us
    ppermute x2 -> x4, starting transfers between devices: 3.11 us -> 4.31 us  [send_rows(): lax.ppermute(outs[j], 'head', [(x, (x + j) % groups) for x in range(group...]
  transfers between devices with their start and end apart: 14 -> 13, of which waited for: 6 -> 7; matrix products, arithmetic and copies ran while one was open for 0% -> 0% of each run, Pallas kernels for 15% -> 20%
where the time goes in v3:
time: 71.8 us; the launch traced here: 71.6 us
  waiting for transfers between devices  35 us (49%)
  Pallas kernels  22.1 us (31%)
  starting transfers between devices  13.1 us (18%)
  between operations  0.76 us (1%)
    ppermute x4, waiting for transfers between devices, send_rows(): lax.ppermute(outs[j], 'head', [(x, (x + j) % groups) for x in range(group...  20.9 us
    pallas_call x4, Pallas kernels, shards(): pl.pallas_call(functools.partial(grad_kernel, heads=2, groups=groups, **s...  11.3 us
    ppermute x4, waiting for transfers between devices, swap_pairs(): lax.ppermute(sent[2 * (hop - 1) + turn], 'seq', perm + [(b, a) for a, b i...  11.1 us
    ppermute x4, starting transfers between devices, swap_pairs(): lax.ppermute(sent[2 * (hop - 1) + turn], 'seq', perm + [(b, a) for a, b i...  7.3 us
    pallas_call x1, Pallas kernels, shards(): pl.pallas_call(functools.partial(state_kernel, heads=group, **sizes), gri...  5.19 us
    ppermute x4, starting transfers between devices, send_rows(): lax.ppermute(outs[j], 'head', [(x, (x + j) % groups) for x in range(group...  4.31 us
    pallas_call x4, Pallas kernels, shards(): pl.pallas_call(functools.partial(place_kernel, groups=groups, offset=offs...  3.68 us
    ppermute x5, waiting for transfers between devices, swap_cores(): return lax.ppermute(a, 'seq', [(b, b ^ 1) for b in range(seq)])  3.02 us
  transfers between devices with their start and end apart: 13, of which 7 were waited for; matrix products, arithmetic and copies ran while one was open for 0% of the time, Pallas kernels for 20%

profile of v3, /device:TPU:0, one launch (start us, length us, event | category | flops | bytes accessed | tf_op | source)
XLA Modules:
  0.0 71.6 jit_solution(5169965734060362572)
XLA Ops:
  0.6 0.0 copy-start.4
  0.6 0.6 copy-done.4
  1.3 5.2 %states.1 = (f32[2,8,128,128]{3,2,1,0:T(8,128)S(1)}, f32[2,8,128,128]{3,2,1,0:T(8,128)}) custom-call(s32[8]{0:T(128)S(1)} %copy-done.4, bf16[256,2048]{1,0:T(8,128)(2,1)} %q.9, bf16[256,2048]{1,0:T(8,128)(2,1)} %k.9, bf16[256,2048]{1,0:T(8,128)(2,1)} %v.9, bf16[256,2048]{1,0:T(8,128)(2,1)} %g.9), custom_call_target="tpu_custom_call" | custom-call | bytes 1024 | tf_op jit(solution)/shard_map/states/pallas_call | solution.py:251
  6.5 0.5 collective-permute-start
  6.9 2.5 %collective-permute-done.got = f32[2,8,128,128]{3,2,1,0:T(8,128)S(1)} collective-permute-done((f32[2,8,128,128]{3,2,1,0:T(8,128)}, f32[2,8,128,128]{3,2,1,0:T(8,128)S(1)}, u32[]{:S(2)}, u32[]{:S(2)}) %collective-permute-start) | collective-permute-done | bytes 1048608 | tf_op jit(solution)/shard_map/ppermute | solution.py:232
  9.4 0.0 copy-start.3
  9.4 0.8 %pair.1 = (bf16[8,128,128]{2,1,0:T(8,128)(2,1)S(1)}, bf16[8,128,128]{2,1,0:T(8,128)(2,1)S(1)}, bf16[8,128,128]{2,1,0:T(8,128)(2,1)S(1)}, bf16[8,128,128]{2,1,0:T(8,128)(2,1)S(1)}) custom-call(s32[8]{0:T(128)S(1)} %copy-done.4, f32[2,8,128,128]{3,2,1,0:T(8,128)S(1)} %get-tuple-element.34.kept, f32[2,8,128,128]{3,2,1,0:T(8,128)S(1)} %collective-permute-done.got), custom_call_target="tpu_custom_call" | custom-call | bytes 1024 | tf_op jit(solution)/shard_map/pair/pallas_call | solution.py:225
  10.2 3.0 %collective-permute-start.1 = (bf16[8,128,128]{2,1,0:T(8,128)(2,1)S(1)}, bf16[8,128,128]{2,1,0:T(8,128)(2,1)S(1)}, u32[]{:S(2)}, u32[]{:S(2)}) collective-permute-start(bf16[8,128,128]{2,1,0:T(8,128)(2,1)S(1)} %get-tuple-element.36), channel_id=1, source_target_pairs={{0,4},{2,6},{8,12},{10,14},{16,20},{18,22},{24,28},{26,30},{4,0},{... | collective-permute-start | bytes 786440 | tf_op jit(solution)/shard_map/ppermute | solution.py:240
  13.2 0.7 collective-permute-start.2
  13.9 0.0 copy-start.5
  13.9 2.9 %collective-permute-start.3 = (bf16[8,128,128]{2,1,0:T(8,128)(2,1)S(1)}, bf16[8,128,128]{2,1,0:T(8,128)(2,1)S(1)}, u32[]{:S(2)}, u32[]{:S(2)}) collective-permute-start(bf16[8,128,128]{2,1,0:T(8,128)(2,1)S(1)} %get-tuple-element.38), channel_id=1, source_target_pairs={{0,8},{2,10},{4,12},{6,14},{16,24},{18,26},{20,28},{22,30},{8,0},{... | collective-permute-start | bytes 786440 | tf_op jit(solution)/shard_map/ppermute | solution.py:240
  16.8 0.0 copy-start
  16.8 0.0 copy-start.1
  16.8 0.0 copy-start.2
  16.8 0.8 %collective-permute-start.4 = (bf16[8,128,128]{2,1,0:T(8,128)(2,1)S(1)}, bf16[8,128,128]{2,1,0:T(8,128)(2,1)S(1)}, u32[]{:S(2)}, u32[]{:S(2)}) collective-permute-start(bf16[8,128,128]{2,1,0:T(8,128)(2,1)S(1)} %get-tuple-element.39), channel_id=1, source_target_pairs={{8,16},{10,18},{12,20},{14,22},{16,8},{18,10},{20,12},{22,14},{9,1... | collective-permute-start | bytes 786440 | tf_op jit(solution)/shard_map/ppermute | solution.py:240
  17.6 7.1 %collective-permute-done.1.rest_0_ = bf16[8,128,128]{2,1,0:T(8,128)(2,1)S(1)} collective-permute-done((bf16[8,128,128]{2,1,0:T(8,128)(2,1)S(1)}, bf16[8,128,128]{2,1,0:T(8,128)(2,1)S(1)}, u32[]{:S(2)}, u32[]{:S(2)}) %collective-permute-start.1) | collective-permute-done | bytes 262176 | tf_op jit(solution)/shard_map/ppermute | solution.py:240
  24.7 0.0 collective-permute-done.2.rest_1_
  24.7 4.0 %collective-permute-done.3.rest_2_ = bf16[8,128,128]{2,1,0:T(8,128)(2,1)S(1)} collective-permute-done((bf16[8,128,128]{2,1,0:T(8,128)(2,1)S(1)}, bf16[8,128,128]{2,1,0:T(8,128)(2,1)S(1)}, u32[]{:S(2)}, u32[]{:S(2)}) %collective-permute-start.3) | collective-permute-done | bytes 262176 | tf_op jit(solution)/shard_map/ppermute | solution.py:240
  28.7 0.0 collective-permute-done.4.rest_3_
  28.7 0.0 copy-done.5
  28.7 1.1 %join.1 = (f32[2,2,128,128]{3,2,1,0:T(8,128)S(1)}, f32[2,2,128,128]{3,2,1,0:T(8,128)S(1)}, f32[2,2,128,128]{3,2,1,0:T(8,128)S(1)}, f32[2,2,128,128]{3,2,1,0:T(8,...) custom-call(s32[8]{0:T(128)S(1)} %copy-done.5, ...), custom_call_target="tpu_custom_call" | custom-call | bytes 1024 | tf_op jit(solution)/shard_map/join/pallas_call | solution.py:225
  29.8 0.1 collective-permute-start.8
  29.9 0.5 collective-permute-start.7
  30.4 0.1 collective-permute-start.6
  30.4 0.4 collective-permute-start.5
  30.9 0.5 collective-permute-done.8.got
  31.4 0.0 copy-done.3
  31.4 0.0 copy-done
  31.4 0.0 copy-done.1
  31.4 0.0 copy-done.2
  31.4 2.8 %grads.4 = (bf16[3,128,512]{2,1,0:T(8,128)(2,1)S(1)}, bf16[3,128,512]{2,1,0:T(8,128)(2,1)S(1)}) custom-call(s32[8]{0:T(128)S(1)} %copy-done.5, bf16[256,2048]{1,0:T(8,128)(2,1)S(1)} %copy-done, bf16[256,2048]{1,0:T(8,128)(2,1)S(1)} %copy-done.1, bf16[256,2048]{1,0:T(8,128)(2,1)S(1)} %copy-done.2, bf16[256,2048]{1,0:T(8,128)(2,1)S(1)} %copy-done.3, ...), custom_call_target="tpu_custom_call" | custom-call | bytes 1024 | tf_op jit(solution)/shard_map/grads/pallas_call | solution.py:276
  34.2 1.7 %collective-permute-start.12 = (bf16[3,128,512]{2,1,0:T(8,128)(2,1)S(1)}, bf16[3,128,512]{2,1,0:T(8,128)(2,1)S(1)}, u32[]{:S(2)}, u32[]{:S(2)}) collective-permute-start(bf16[3,128,512]{2,1,0:T(8,128)(2,1)S(1)} %get-tuple-element.55), channel_id=1, source_target_pairs={{0,1},{1,0},{2,3},{3,2},{4,5},{5,4},{6,7},{7,6},{8,9},{9,8},{10,11... | collective-permute-start | bytes 1179656 | tf_op jit(solution)/shard_map/ppermute | solution.py:246
  35.9 0.0 collective-permute-done.7.got
  35.9 2.8 %grads.5 = (bf16[3,128,512]{2,1,0:T(8,128)(2,1)S(1)}, bf16[3,128,512]{2,1,0:T(8,128)(2,1)S(1)}) custom-call(s32[8]{0:T(128)S(1)} %copy-done.5, bf16[256,2048]{1,0:T(8,128)(2,1)S(1)} %copy-done, bf16[256,2048]{1,0:T(8,128)(2,1)S(1)} %copy-done.1, bf16[256,2048]{1,0:T(8,128)(2,1)S(1)} %copy-done.2, bf16[256,2048]{1,0:T(8,128)(2,1)S(1)} %copy-done.3, ...), custom_call_target="tpu_custom_call" | custom-call | bytes 1024 | tf_op jit(solution)/shard_map/grads/pallas_call | solution.py:276
  38.7 0.5 collective-permute-start.11
  39.2 0.0 collective-permute-done.6.got
  39.2 2.8 %grads.6 = (bf16[3,128,512]{2,1,0:T(8,128)(2,1)S(1)}, bf16[3,128,512]{2,1,0:T(8,128)(2,1)S(1)}) custom-call(s32[8]{0:T(128)S(1)} %copy-done.5, bf16[256,2048]{1,0:T(8,128)(2,1)S(1)} %copy-done, bf16[256,2048]{1,0:T(8,128)(2,1)S(1)} %copy-done.1, bf16[256,2048]{1,0:T(8,128)(2,1)S(1)} %copy-done.2, bf16[256,2048]{1,0:T(8,128)(2,1)S(1)} %copy-done.3, ...), custom_call_target="tpu_custom_call" | custom-call | bytes 1024 | tf_op jit(solution)/shard_map/grads/pallas_call | solution.py:276
  42.0 1.7 %collective-permute-start.10 = (bf16[3,128,512]{2,1,0:T(8,128)(2,1)S(1)}, bf16[3,128,512]{2,1,0:T(8,128)(2,1)S(1)}, u32[]{:S(2)}, u32[]{:S(2)}) collective-permute-start(bf16[3,128,512]{2,1,0:T(8,128)(2,1)S(1)} %get-tuple-element.53), channel_id=1, source_target_pairs={{0,1},{1,0},{2,3},{3,2},{4,5},{5,4},{6,7},{7,6},{8,9},{9,8},{10,11... | collective-permute-start | bytes 1179656 | tf_op jit(solution)/shard_map/ppermute | solution.py:246
  43.7 0.0 collective-permute-done.5.got
  43.7 2.8 %grads.7 = (bf16[3,128,512]{2,1,0:T(8,128)(2,1)S(1)}, bf16[3,128,512]{2,1,0:T(8,128)(2,1)S(1)}) custom-call(s32[8]{0:T(128)S(1)} %copy-done.5, bf16[256,2048]{1,0:T(8,128)(2,1)S(1)} %copy-done, bf16[256,2048]{1,0:T(8,128)(2,1)S(1)} %copy-done.1, bf16[256,2048]{1,0:T(8,128)(2,1)S(1)} %copy-done.2, bf16[256,2048]{1,0:T(8,128)(2,1)S(1)} %copy-done.3, ...), custom_call_target="tpu_custom_call" | custom-call | bytes 1024 | tf_op jit(solution)/shard_map/grads/pallas_call | solution.py:276
  46.5 0.5 collective-permute-start.9
  47.0 0.0 collective-permute-done.12.refs_1_
  47.0 0.9 %place.4 = (bf16[128,4096]{1,0:T(8,128)(2,1)}, bf16[128,4096]{1,0:T(8,128)(2,1)}, bf16[128,4096]{1,0:T(8,128)(2,1)}) custom-call(bf16[3,128,512]{2,1,0:T(8,128)(2,1)S(1)} %get-tuple-element.48.rest_0_.refs_0_, bf16[3,128,512]{2,1,0:T(8,128)(2,1)S(1)} %collective-permute-done.12.refs_1_), custom_call_target="tpu_custom_call" | custom-call | bytes 1024 | tf_op jit(solution)/shard_map/place/pallas_call | solution.py:292
  48.0 6.7 %collective-permute-done.11.refs_1_ = bf16[3,128,512]{2,1,0:T(8,128)(2,1)S(1)} collective-permute-done((bf16[3,128,512]{2,1,0:T(8,128)(2,1)S(1)}, bf16[3,128,512]{2,1,0:T(8,128)(2,1)S(1)}, u32[]{:S(2)}, u32[]{:S(2)}) %collective-permute-start.11) | collective-permute-done | bytes 393248 | tf_op jit(solution)/shard_map/ppermute | solution.py:246
  54.7 0.9 %place.5 = (bf16[128,4096]{1,0:T(8,128)(2,1)}, bf16[128,4096]{1,0:T(8,128)(2,1)}, bf16[128,4096]{1,0:T(8,128)(2,1)}) custom-call(bf16[3,128,512]{2,1,0:T(8,128)(2,1)S(1)} %get-tuple-element.49.rest_0_.refs_0_, bf16[3,128,512]{2,1,0:T(8,128)(2,1)S(1)} %collective-permute-done.11.refs_1_, ...), custom_call_target="tpu_custom_call", output_to_operand_aliasing={{0}: (2, {}), {1}: (3, {}), {2}: (4, {})} | custom-call | bytes 1024 | tf_op jit(solution)/shard_map/place/pallas_call | solution.py:292
  55.6 7.5 %collective-permute-done.10.refs_1_ = bf16[3,128,512]{2,1,0:T(8,128)(2,1)S(1)} collective-permute-done((bf16[3,128,512]{2,1,0:T(8,128)(2,1)S(1)}, bf16[3,128,512]{2,1,0:T(8,128)(2,1)S(1)}, u32[]{:S(2)}, u32[]{:S(2)}) %collective-permute-start.10) | collective-permute-done | bytes 393248 | tf_op jit(solution)/shard_map/ppermute | solution.py:246
  63.1 0.9 %place.6 = (bf16[128,4096]{1,0:T(8,128)(2,1)}, bf16[128,4096]{1,0:T(8,128)(2,1)}, bf16[128,4096]{1,0:T(8,128)(2,1)}) custom-call(bf16[3,128,512]{2,1,0:T(8,128)(2,1)S(1)} %get-tuple-element.50.rest_0_.refs_0_, bf16[3,128,512]{2,1,0:T(8,128)(2,1)S(1)} %collective-permute-done.10.refs_1_, ...), custom_call_target="tpu_custom_call", output_to_operand_aliasing={{0}: (2, {}), {1}: (3, {}), {2}: (4, {})} | custom-call | bytes 1024 | tf_op jit(solution)/shard_map/place/pallas_call | solution.py:292
  64.0 6.7 %collective-permute-done.9.refs_1_ = bf16[3,128,512]{2,1,0:T(8,128)(2,1)S(1)} collective-permute-done((bf16[3,128,512]{2,1,0:T(8,128)(2,1)S(1)}, bf16[3,128,512]{2,1,0:T(8,128)(2,1)S(1)}, u32[]{:S(2)}, u32[]{:S(2)}) %collective-permute-start.9) | collective-permute-done | bytes 393248 | tf_op jit(solution)/shard_map/ppermute | solution.py:246
  70.7 0.9 %place.7 = (bf16[128,4096]{1,0:T(8,128)(2,1)}, bf16[128,4096]{1,0:T(8,128)(2,1)}, bf16[128,4096]{1,0:T(8,128)(2,1)}) custom-call(bf16[3,128,512]{2,1,0:T(8,128)(2,1)S(1)} %get-tuple-element.51.refs_0_, bf16[3,128,512]{2,1,0:T(8,128)(2,1)S(1)} %collective-permute-done.9.refs_1_, ...), custom_call_target="tpu_custom_call", output_to_operand_aliasing={{0}: (2, {}), {1}: (3, {}), {2}: (4, {})} | custom-call | bytes 1024 | tf_op jit(solution)/shard_map/place/pallas_call | solution.py:292
Async XLA Ops:
  0.6 0.7 copy-start.4
  6.5 3.0 %collective-permute-start = (f32[2,8,128,128]{3,2,1,0:T(8,128)}, f32[2,8,128,128]{3,2,1,0:T(8,128)S(1)}, u32[]{:S(2)}, u32[]{:S(2)}) collective-permute-start(f32[2,8,128,128]{3,2,1,0:T(8,128)} %get-tuple-element.35), channel_id=1, source_target_pairs={{0,2},{2,0},{4,6},{6,4},{8,10},{10,8},{12,14},{14,12},{16,18},{18,... | collective-permute-start | bytes 3145736 | tf_op jit(solution)/shard_map/ppermute | solution.py:232
  9.4 22.0 %copy-start.3 = (bf16[256,2048]{1,0:T(8,128)(2,1)S(1)}, bf16[256,2048]{1,0:T(8,128)(2,1)}, u32[]{:S(2)}) copy-start(bf16[256,2048]{1,0:T(8,128)(2,1)} %g.9) | copy-start | bytes 3145732
  10.2 14.4 %collective-permute-start.1 = (bf16[8,128,128]{2,1,0:T(8,128)(2,1)S(1)}, bf16[8,128,128]{2,1,0:T(8,128)(2,1)S(1)}, u32[]{:S(2)}, u32[]{:S(2)}) collective-permute-start(bf16[8,128,128]{2,1,0:T(8,128)(2,1)S(1)} %get-tuple-element.36), channel_id=1, source_target_pairs={{0,4},{2,6},{8,12},{10,14},{16,20},{18,22},{24,28},{26,30},{4,0},{... | collective-permute-start | bytes 786440 | tf_op jit(solution)/shard_map/ppermute | solution.py:240
  13.2 11.5 %collective-permute-start.2 = (bf16[8,128,128]{2,1,0:T(8,128)(2,1)S(1)}, bf16[8,128,128]{2,1,0:T(8,128)(2,1)S(1)}, u32[]{:S(2)}, u32[]{:S(2)}) collective-permute-start(bf16[8,128,128]{2,1,0:T(8,128)(2,1)S(1)} %get-tuple-element.37), channel_id=1, source_target_pairs={{4,8},{6,10},{12,16},{14,18},{20,24},{22,26},{8,4},{10,6},{16,12},... | collective-permute-start | bytes 786440 | tf_op jit(solution)/shard_map/ppermute | solution.py:240
  13.9 14.8 %copy-start.5 = (s32[8]{0:T(128)S(1)}, s32[8]{0:T(128)}, u32[]{:S(2)}) copy-start(s32[8]{0:T(128)} %lengths.13) | copy-start | bytes 100
  13.9 14.8 %collective-permute-start.3 = (bf16[8,128,128]{2,1,0:T(8,128)(2,1)S(1)}, bf16[8,128,128]{2,1,0:T(8,128)(2,1)S(1)}, u32[]{:S(2)}, u32[]{:S(2)}) collective-permute-start(bf16[8,128,128]{2,1,0:T(8,128)(2,1)S(1)} %get-tuple-element.38), channel_id=1, source_target_pairs={{0,8},{2,10},{4,12},{6,14},{16,24},{18,26},{20,28},{22,30},{8,0},{... | collective-permute-start | bytes 786440 | tf_op jit(solution)/shard_map/ppermute | solution.py:240
  16.8 14.6 %copy-start = (bf16[256,2048]{1,0:T(8,128)(2,1)S(1)}, bf16[256,2048]{1,0:T(8,128)(2,1)}, u32[]{:S(2)}) copy-start(bf16[256,2048]{1,0:T(8,128)(2,1)} %q.9) | copy-start | bytes 3145732
  16.8 14.6 %copy-start.1 = (bf16[256,2048]{1,0:T(8,128)(2,1)S(1)}, bf16[256,2048]{1,0:T(8,128)(2,1)}, u32[]{:S(2)}) copy-start(bf16[256,2048]{1,0:T(8,128)(2,1)} %k.9) | copy-start | bytes 3145732
  16.8 14.6 %copy-start.2 = (bf16[256,2048]{1,0:T(8,128)(2,1)S(1)}, bf16[256,2048]{1,0:T(8,128)(2,1)}, u32[]{:S(2)}) copy-start(bf16[256,2048]{1,0:T(8,128)(2,1)} %v.9) | copy-start | bytes 3145732
  16.8 11.9 %collective-permute-start.4 = (bf16[8,128,128]{2,1,0:T(8,128)(2,1)S(1)}, bf16[8,128,128]{2,1,0:T(8,128)(2,1)S(1)}, u32[]{:S(2)}, u32[]{:S(2)}) collective-permute-start(bf16[8,128,128]{2,1,0:T(8,128)(2,1)S(1)} %get-tuple-element.39), channel_id=1, source_target_pairs={{8,16},{10,18},{12,20},{14,22},{16,8},{18,10},{20,12},{22,14},{9,1... | collective-permute-start | bytes 786440 | tf_op jit(solution)/shard_map/ppermute | solution.py:240
  29.8 1.6 %collective-permute-start.8 = (f32[2,2,128,128]{3,2,1,0:T(8,128)S(1)}, f32[2,2,128,128]{3,2,1,0:T(8,128)S(1)}, u32[]{:S(2)}, u32[]{:S(2)}) collective-permute-start(f32[2,2,128,128]{3,2,1,0:T(8,128)S(1)} %get-tuple-element.47), channel_id=1, source_target_pairs={{0,2},{2,0},{4,6},{6,4},{8,10},{10,8},{12,14},{14,12},{16,18},{18,... | collective-permute-start | bytes 786440 | tf_op jit(solution)/shard_map/ppermute | solution.py:232
  29.9 6.0 %collective-permute-start.7 = (f32[2,2,128,128]{3,2,1,0:T(8,128)S(1)}, f32[2,2,128,128]{3,2,1,0:T(8,128)S(1)}, u32[]{:S(2)}, u32[]{:S(2)}) collective-permute-start(f32[2,2,128,128]{3,2,1,0:T(8,128)S(1)} %get-tuple-element.45), channel_id=1, source_target_pairs={{0,2},{2,0},{4,6},{6,4},{8,10},{10,8},{12,14},{14,12},{16,18},{18,... | collective-permute-start | bytes 786440 | tf_op jit(solution)/shard_map/ppermute | solution.py:232
  30.4 8.8 %collective-permute-start.6 = (f32[2,2,128,128]{3,2,1,0:T(8,128)S(1)}, f32[2,2,128,128]{3,2,1,0:T(8,128)S(1)}, u32[]{:S(2)}, u32[]{:S(2)}) collective-permute-start(f32[2,2,128,128]{3,2,1,0:T(8,128)S(1)} %get-tuple-element.43), channel_id=1, source_target_pairs={{0,2},{2,0},{4,6},{6,4},{8,10},{10,8},{12,14},{14,12},{16,18},{18,... | collective-permute-start | bytes 786440 | tf_op jit(solution)/shard_map/ppermute | solution.py:232
  30.4 13.3 %collective-permute-start.5 = (f32[2,2,128,128]{3,2,1,0:T(8,128)S(1)}, f32[2,2,128,128]{3,2,1,0:T(8,128)S(1)}, u32[]{:S(2)}, u32[]{:S(2)}) collective-permute-start(f32[2,2,128,128]{3,2,1,0:T(8,128)S(1)} %get-tuple-element.41), channel_id=1, source_target_pairs={{0,2},{2,0},{4,6},{6,4},{8,10},{10,8},{12,14},{14,12},{16,18},{18,... | collective-permute-start | bytes 786440 | tf_op jit(solution)/shard_map/ppermute | solution.py:232
  34.2 12.8 %collective-permute-start.12 = (bf16[3,128,512]{2,1,0:T(8,128)(2,1)S(1)}, bf16[3,128,512]{2,1,0:T(8,128)(2,1)S(1)}, u32[]{:S(2)}, u32[]{:S(2)}) collective-permute-start(bf16[3,128,512]{2,1,0:T(8,128)(2,1)S(1)} %get-tuple-element.55), channel_id=1, source_target_pairs={{0,1},{1,0},{2,3},{3,2},{4,5},{5,4},{6,7},{7,6},{8,9},{9,8},{10,11... | collective-permute-start | bytes 1179656 | tf_op jit(solution)/shard_map/ppermute | solution.py:246
  38.7 16.0 %collective-permute-start.11 = (bf16[3,128,512]{2,1,0:T(8,128)(2,1)S(1)}, bf16[3,128,512]{2,1,0:T(8,128)(2,1)S(1)}, u32[]{:S(2)}, u32[]{:S(2)}) collective-permute-start(bf16[3,128,512]{2,1,0:T(8,128)(2,1)S(1)} %get-tuple-element.54), channel_id=1, source_target_pairs={{0,1},{1,0},{2,3},{3,2},{4,5},{5,4},{6,7},{7,6},{8,9},{9,8},{10,11... | collective-permute-start | bytes 1179656 | tf_op jit(solution)/shard_map/ppermute | solution.py:246
  42.0 21.1 %collective-permute-start.10 = (bf16[3,128,512]{2,1,0:T(8,128)(2,1)S(1)}, bf16[3,128,512]{2,1,0:T(8,128)(2,1)S(1)}, u32[]{:S(2)}, u32[]{:S(2)}) collective-permute-start(bf16[3,128,512]{2,1,0:T(8,128)(2,1)S(1)} %get-tuple-element.53), channel_id=1, source_target_pairs={{0,1},{1,0},{2,3},{3,2},{4,5},{5,4},{6,7},{7,6},{8,9},{9,8},{10,11... | collective-permute-start | bytes 1179656 | tf_op jit(solution)/shard_map/ppermute | solution.py:246
  46.5 24.2 %collective-permute-start.9 = (bf16[3,128,512]{2,1,0:T(8,128)(2,1)S(1)}, bf16[3,128,512]{2,1,0:T(8,128)(2,1)S(1)}, u32[]{:S(2)}, u32[]{:S(2)}) collective-permute-start(bf16[3,128,512]{2,1,0:T(8,128)(2,1)S(1)} %get-tuple-element.52), channel_id=1, source_target_pairs={{0,1},{1,0},{2,3},{3,2},{4,5},{5,4},{6,7},{7,6},{8,9},{9,8},{10,11... | collective-permute-start | bytes 1179656 | tf_op jit(solution)/shard_map/ppermute | solution.py:246
